TPU v7x, 128 devices: a whole 4x4x4 slice. The times are simulated.
128 devices in a mesh: grp: 4 (over y_hi, core), gx: 8 (over z, y_lo), gy: 4 (over x).
Axes of the slice: x: 4, y: 4 (y_hi: 2, y_lo: 2; y = y_hi * 2 + y_lo), z: 4, core: 2. Of those that a mesh axis runs over, the one named last changes fastest.
Arguments:
- fields: float32 [4, 5, 128, 128, 384], P('grp', None, 'gx', 'gy'), may hold values from -6 to 6
- closure_in: float32 [64, 5], replicated, may hold values from -2.5 to 2.5
- closure_bias: float32 [64], replicated, may hold values from -4 to 4
- closure_out: float32 [64], replicated, may hold values from -0.75 to 0.75
- master: float32 [17280], replicated, may hold values from -0.6 to 0.6
- momentum: float32 [17280], replicated, may hold values from -3 to 3
- sample_block: int32 [96], replicated, may hold values from 0 to 47
- sample_trainer: int32 [96], replicated, may hold values from 0 to 31, as said below
Outputs:
- new_fields: float32 [4, 5, 128, 128, 384], P('grp', None, 'gx', 'gy')
- new_master: float32 [17280], P(('grp', 'gx', 'gy'))
- new_momentum: float32 [17280], P(('grp', 'gx', 'gy'))
Inputs may be any that keep to these rules, and one draw needn't show every extreme that they name: `sample_trainer`: entry o names the trainer c = gx * 4 + gy of the last group that receives the cube of evolution device o. Every trainer receives at least 2 and at most 6 cubes, at most 4 from one evolution group; in every draw some trainer receives 6, 4 of them from one group.
All inputs are finite; a program needn't handle non-finite values.
Results may differ from a plain program's by a relative error of at most 0.0026.
The roundings to bfloat16 on the way count: a program that leaves them out, or rounds other values in their place, can miss the bound.
Values may be sent and summed in bfloat16 or wider, within the bound.
A program may use at most 192 MiB of HBM per device.

v0:
```python
import jax
import jax.numpy as jnp
from jax import lax
from jax.sharding import PartitionSpec as P

F = 5
CH = 64
SUB = 16
TCAP = 6
INNER = 3
CELLS = 4096
NPARAM = 17280


time_step = 0.1
base_viscosity = 0.02
viscosity_gain = 0.2
buoyancy = 0.5
inner_rate = 0.02
outer_rate = 0.01
momentum_decay = 0.9
norm_epsilon = 1e-06
highest = lax.Precision.HIGHEST


def with_halo(cells, sides, width):
    for axis, dim in sides:
        count = lax.axis_size(axis)
        head = lax.slice_in_dim(cells, 0, width, axis=dim)
        tail = lax.slice_in_dim(cells, cells.shape[dim] - width, cells.shape[dim], axis=dim)
        cells = jnp.concatenate(
            [
                lax.ppermute(tail, axis, [(i, (i + 1) % count) for i in range(count)]),
                cells,
                lax.ppermute(head, axis, [((i + 1) % count, i) for i in range(count)]),
            ],
            axis=dim,
        )
    return cells


def spread(block, axis, owner):
    block = jnp.where(lax.axis_index(axis) == owner, block, jnp.zeros_like(block))
    return lax.psum(block, axis)


def eddy_viscosity(center, closure_in, closure_bias, closure_out):
    channels, x_cells, y_cells, z_cells = center.shape
    flattened = center.reshape(channels, x_cells * y_cells * z_cells)
    block_size = 4 * y_cells * z_cells
    block_count = x_cells // 4

    def viscosity_block(block_index):
        columns = lax.dynamic_slice_in_dim(flattened, block_index * block_size, block_size, 1)
        hidden = jax.nn.silu(
            jnp.dot(closure_in, columns, precision=highest) + closure_bias[:, None]
        )
        return viscosity_gain * jax.nn.softplus(jnp.dot(closure_out, hidden, precision=highest))

    blocks = lax.map(viscosity_block, jnp.arange(block_count, dtype=jnp.int32))
    return blocks.reshape(x_cells, y_cells, z_cells)


def field_tendency(padded, closure_in, closure_bias, closure_out):
    walled = jnp.pad(padded, ((0, 0), (0, 0), (0, 0), (1, 1)))
    center = walled[:, 1:-1, 1:-1, 1:-1]
    east_side = walled[:, 2:, 1:-1, 1:-1]
    west_side = walled[:, :-2, 1:-1, 1:-1]
    north_side = walled[:, 1:-1, 2:, 1:-1]
    south_side = walled[:, 1:-1, :-2, 1:-1]
    upper_side = walled[:, 1:-1, 1:-1, 2:]
    lower_side = walled[:, 1:-1, 1:-1, :-2]
    laplacian = (
        east_side + west_side + north_side + south_side + upper_side + lower_side - 6.0 * center
    )
    advection = (
        center[0] * (east_side - west_side)
        + center[1] * (north_side - south_side)
        + center[2] * (upper_side - lower_side)
    )
    viscosity = base_viscosity + eddy_viscosity(center, closure_in, closure_bias, closure_out)
    tendency = viscosity * laplacian - 0.5 * advection
    return tendency.at[2].add(buoyancy * center[3])


def shift_tables(edge_cells, slot_count):
    cube_cells = edge_cells * edge_cells * edge_cells
    position = jnp.arange(slot_count * cube_cells, dtype=jnp.int32) % cube_cells
    x_coord = position // (edge_cells * edge_cells)
    y_coord = position // edge_cells % edge_cells
    z_coord = position % edge_cells
    tables = []
    for x_step in (-1, 0, 1):
        for y_step in (-1, 0, 1):
            for z_step in (-1, 0, 1):
                offset = x_step * edge_cells * edge_cells + y_step * edge_cells + z_step
                inside = (x_coord + x_step >= 0) & (x_coord + x_step < edge_cells)
                inside = inside & (y_coord + y_step >= 0) & (y_coord + y_step < edge_cells)
                inside = inside & (z_coord + z_step >= 0) & (z_coord + z_step < edge_cells)
                tables.append((offset, inside))
    return tables


def shift_from(values, offset, inside):
    return jnp.where(inside, jnp.roll(values, -offset, axis=1), jnp.zeros((), values.dtype))


def shift_back(values, offset, inside):
    return jnp.roll(jnp.where(inside, values, jnp.zeros((), values.dtype)), offset, axis=1)


def stacked_from(values, tables):
    return jnp.concatenate(
        [shift_from(values, offset, inside) for offset, inside in tables], axis=0
    )


def stacked_back(values, tables):
    return jnp.concatenate(
        [shift_back(values, offset, inside) for offset, inside in tables], axis=0
    )


def silu_slope(values):
    sigmoid_value = jax.nn.sigmoid(values)
    return sigmoid_value * (1.0 + values * (1.0 - sigmoid_value))


def batch_gradient(flat_weights, inputs, targets, cell_weight, tables):
    first_count = CH * 27 * F
    first_weight = flat_weights[:first_count].reshape(CH, 27 * F)
    last_weight = flat_weights[first_count:].reshape(F, 27, CH)
    stacked_last = jnp.transpose(last_weight, (1, 0, 2)).reshape(27 * F, CH)
    input_stack = stacked_from(inputs, tables)
    first_pre = jnp.dot(first_weight, input_stack, preferred_element_type=jnp.float32)
    hidden = jax.nn.silu(first_pre).astype(jnp.bfloat16)
    partial_out = jnp.dot(stacked_last, hidden, preferred_element_type=jnp.float32)
    predicted = jnp.zeros((F, inputs.shape[1]), jnp.float32)
    for slot_index, (offset, inside) in enumerate(tables):
        predicted = predicted + shift_from(
            partial_out[slot_index * F : (slot_index + 1) * F], offset, inside
        )
    error_grad = (2.0 * cell_weight[None, :] * (predicted - targets.astype(jnp.float32))).astype(
        jnp.bfloat16
    )
    grad_stack = stacked_back(error_grad, tables)
    last_grad = lax.dot_general(
        grad_stack, hidden, (((1,), (1,)), ((), ())), preferred_element_type=jnp.float32
    )
    last_grad = jnp.transpose(last_grad.reshape(27, F, CH), (1, 0, 2)).reshape(F * 27 * CH)
    hidden_grad = lax.dot_general(
        stacked_last, grad_stack, (((0,), (0,)), ((), ())), preferred_element_type=jnp.float32
    )
    pre_grad = (hidden_grad * silu_slope(first_pre)).astype(jnp.bfloat16)
    first_grad = lax.dot_general(
        pre_grad, input_stack, (((1,), (1,)), ((), ())), preferred_element_type=jnp.float32
    )
    return jnp.concatenate([first_grad.reshape(CH * 27 * F), last_grad])


def local_train(flat_weights, inputs, targets, cell_weight, tables):
    start_weights = flat_weights.astype(jnp.float32)
    current = start_weights
    for inner_index in range(INNER):
        gradient = batch_gradient(
            current.astype(jnp.bfloat16), inputs, targets, cell_weight, tables
        )
        current = current - inner_rate * gradient
    return start_weights - current


def slot_lists(sample_trainer, column):
    owner_ids = jnp.arange(sample_trainer.shape[0], dtype=jnp.int32)
    same_trainer = sample_trainer[:, None] == sample_trainer[None, :]
    earlier = owner_ids[None, :] < owner_ids[:, None]
    rank_all = jnp.sum((same_trainer & earlier).astype(jnp.int32), axis=1)
    mine_mask = sample_trainer == column
    slot_ids = jnp.arange(TCAP, dtype=jnp.int32)
    chosen = mine_mask[None, :] & (rank_all[None, :] == slot_ids[:, None])
    slot_owner = jnp.sum(jnp.where(chosen, owner_ids[None, :], 0), axis=1)
    slot_valid = jnp.any(chosen, axis=1)
    sample_count = jnp.maximum(jnp.sum(mine_mask.astype(jnp.int32)), 1)
    return (slot_owner, slot_valid, sample_count)


def train_batch(batch_cubes, slot_valid, sample_count, flat_weights, tables):
    inputs = jnp.transpose(batch_cubes[:, :F], (1, 0, 2)).reshape(F, TCAP * CELLS)
    targets = jnp.transpose(batch_cubes[:, F:], (1, 0, 2)).reshape(F, TCAP * CELLS)
    slot_weight = jnp.where(slot_valid, 1.0 / (sample_count.astype(jnp.float32) * CELLS), 0.0)
    cell_weight = jnp.repeat(slot_weight, CELLS)
    return local_train(flat_weights, inputs, targets, cell_weight, tables)


def on_device(
    fields, closure_in, closure_bias, closure_out, master, momentum, sample_block, sample_trainer
):
    group_count = lax.axis_size("grp")
    y_devices = lax.axis_size("gy")
    trainers = lax.axis_size("gx") * y_devices
    my_group = lax.axis_index("grp")
    my_column = lax.axis_index("gx") * y_devices + lax.axis_index("gy")
    is_trainer = my_group == group_count - 1
    own_brick = fields[0]
    flat_weights = master.astype(jnp.bfloat16)
    padded = with_halo(own_brick, (("gx", 1), ("gy", 2)), 1)

    def evolve():
        return field_tendency(padded, closure_in, closure_bias, closure_out)

    def stand_aside():
        return jnp.zeros_like(own_brick)

    tendency = lax.cond(is_trainer, stand_aside, evolve)
    new_fields = (own_brick + time_step * tendency)[None]
    sim_group = jnp.minimum(my_group, group_count - 2)
    owner_id = sim_group * trainers + my_column
    block_id = sample_block[owner_id]
    destination = sample_trainer[owner_id]
    y_blocks = own_brick.shape[2] // SUB
    z_blocks = own_brick.shape[3] // SUB
    corner = (
        jnp.int32(0),
        block_id // (y_blocks * z_blocks) * SUB,
        block_id // z_blocks % y_blocks * SUB,
        block_id % z_blocks * SUB,
    )
    old_cube = lax.dynamic_slice(own_brick, corner, (F, SUB, SUB, SUB)).reshape(F, CELLS)
    new_cube = lax.dynamic_slice(tendency, corner, (F, SUB, SUB, SUB)).reshape(F, CELLS)
    payload = jnp.concatenate(
        [old_cube.astype(jnp.bfloat16), new_cube.astype(jnp.bfloat16)], axis=0
    )
    payload = jnp.where(is_trainer, jnp.zeros_like(payload), payload)
    slot_owner, slot_valid, sample_count = slot_lists(sample_trainer, my_column)
    zero_value = jnp.zeros((), jnp.bfloat16)
    device_ids = jnp.arange(group_count * trainers, dtype=jnp.int32)
    wanted = device_ids == (group_count - 1) * trainers + destination
    outgoing = jnp.where(wanted[:, None, None], payload[None], zero_value)
    arrived = lax.all_to_all(outgoing, ("grp", "gx", "gy"), split_axis=0, concat_axis=0, tiled=True)
    gathered_cubes = jnp.take(arrived, slot_owner, axis=0)
    batch_cubes = jnp.where(slot_valid[:, None, None], gathered_cubes, zero_value)
    tables = shift_tables(SUB, TCAP)

    def train_here():
        return train_batch(batch_cubes, slot_valid, sample_count, flat_weights, tables)

    def skip_training():
        return jnp.zeros((NPARAM,), jnp.float32)

    weight_delta = lax.cond(is_trainer, train_here, skip_training)
    share_size = NPARAM // (group_count * trainers)
    share_start = (my_group * trainers + my_column) * share_size
    momentum_share = lax.dynamic_slice_in_dim(momentum, share_start, share_size)
    master_share = lax.dynamic_slice_in_dim(master, share_start, share_size)
    group_delta = lax.psum(weight_delta, ("gx", "gy"))
    total_delta = spread(group_delta, "grp", group_count - 1)
    inverse = 1.0 / jnp.sqrt(jnp.sum(total_delta * total_delta) / NPARAM + norm_epsilon)
    delta_share = lax.dynamic_slice_in_dim(total_delta, share_start, share_size)
    new_momentum = momentum_decay * momentum_share + delta_share * inverse
    new_master = master_share - outer_rate * new_momentum
    return (new_fields, new_master, new_momentum)


def solution(mesh):
    in_specs = (P("grp", None, "gx", "gy", None), P(), P(), P(), P(), P(), P(), P())
    out_specs = (P("grp", None, "gx", "gy", None), P(("grp", "gx", "gy")), P(("grp", "gx", "gy")))
    return jax.shard_map(
        on_device, mesh=mesh, in_specs=in_specs, out_specs=out_specs, check_vma=False
    )
```

profile of v0, /device:TPU:1, one launch (start us, length us, event | category | flops | bytes accessed | tf_op | source)
XLA Modules:
  0.0 1597.5 jit_solution(11744602495485805915)
XLA Ops:
  8.3 2.2 collective-permute-start
  10.5 3.6 collective-permute-start.1
  17.3 2.4 collective-permute-done
  19.6 3.0 collective-permute-done.1
  22.6 1.7 pad_maximum_fusion.81
  30.1 5.0 pad_maximum_fusion.78
  35.1 138.9 %conditional.2 = (f32[5,16,32,384]{3,2,1,0:T(8,128)}) conditional(s32[]{:T(128)} %convert_element_type.138, (f32[5,18,34,384]{3,2,1,0:T(8,128)}, f32[64,5]{0,1:T(8,128)S(1)}, f32[64]{0:T(128)S(1)}, f32[64]{0:T(128)S(1)}) %tuple.910, () %tuple.104), branch_computations={%region_0.3_spmd, %region_3.4_spmd} | conditional | flops 260849664 | bytes 85944368 | solution.py:213
  35.2 2.1 slice_bitcast_fusion.2
  37.3 3.0 slice.2810
  40.3 5.1 copy.38
  45.4 107.5 %while.10 = (s32[]{:T(128)}, f32[4,49152]{1,0:T(4,128)}, s32[4]{0:T(128)S(1)}, f32[5,196608]{1,0:T(8,128)}, f32[64,5]{0,1:T(8,128)S(1)}, /*index=5*/f32[64]{0:T(...) while((s32[]{:T(128)}, f32[4,49152]{1,0:T(4,128)}, s32[4]{0:T(128)S(1)}, ...), condition=%wide.region_2.2_spmd, body=%wide.region_1.1_spmd.sunk | while | flops 242565120 | bytes 27723704 | solution.py:60
  46.8 11.5 fusion.400
  58.4 9.2 fusion.401
  67.7 4.7 dynamic_update_slice.5
  73.6 11.5 fusion.400
  85.2 9.2 fusion.401
  94.5 4.7 dynamic_update_slice.5
  100.4 11.5 fusion.400
  112.0 9.2 fusion.401
  121.3 4.7 dynamic_update_slice.5
  127.2 11.5 fusion.400
  138.8 9.2 fusion.401
  148.1 4.7 dynamic_update_slice.5
  155.8 15.4 multiply_subtract_fusion
  171.2 2.4 fusion.13
  175.8 6.1 broadcast_select_fusion.82
  181.9 12.3 all-to-all-start
  194.5 244.2 %all-to-all-done = bf16[128,10,4096]{2,1,0:T(8,128)(2,1)} async-done(((bf16[128,10,4096]{2,1,0:T(8,128)(2,1)}), bf16[128,10,4096]{2,1,0:T(8,128)(2,1)}, u32[]{:S(2)}, u32[]{:S(2)}) %all-to-all-start) | async-done | bytes 10485792 | tf_op jit(solution)/shard_map/all_to_all | solution.py:238
  438.8 1.8 conditional.3
  441.3 1089.4 %all-reduce.4.cloned.1.call-done = f32[17280]{0:T(1024)} async-done(((f32[17280]{0:T(1024)}), f32[17280]{0:T(1024)}) %all-reduce.4.cloned.1.call-update) | async-done | bytes 69136 | tf_op jit(solution)/shard_map/psum | solution.py:254
  1531.4 6.3 add_bitcast_fusion
  1537.8 49.1 %all-reduce.6.cloned.1.call-done = f32[17280]{0:T(1024)} async-done(((f32[17280]{0:T(1024)}), f32[17280]{0:T(1024)}) %all-reduce.6.cloned.1.call-update) | async-done | bytes 69136 | tf_op jit(solution)/shard_map/psum | solution.py:44
  (59 shorter events, 19.2 us)
Async XLA Ops:
  7.2 21.2 %copy-start.114 = (s32[96]{0:T(128)S(1)}, s32[96]{0:T(128)}, u32[]{:S(2)}) copy-start(s32[96]{0:T(128)} %param.23) | copy-start | bytes 1156
  8.3 11.3 collective-permute-start
  10.5 12.1 collective-permute-start.1
  24.3 10.8 copy-start.18
  24.3 10.8 copy-start.113
  24.4 10.8 copy-start.116
  24.4 5.7 collective-permute-start.2
  25.7 4.4 collective-permute-start.3
  181.9 12.4 copy-start.112
  181.9 12.4 copy-start.115
  181.9 256.9 %all-to-all-start = ((bf16[128,10,4096]{2,1,0:T(8,128)(2,1)}), bf16[128,10,4096]{2,1,0:T(8,128)(2,1)}, u32[]{:S(2)}, u32[]{:S(2)}) async-start(bf16[128,10,4096]{2,1,0:T(8,128)(2,1)} %broadcast_select_fusion.82), calls=%async_computation | async-start | bytes 33554432 | tf_op jit(solution)/shard_map/all_to_all | solution.py:238
  194.2 1336.5 %all-reduce.4.cloned.1.call-start = ((), (), s32[]{:S(2)}) async-start(), calls=%async_computation.1 | async-start | bytes 139264 | tf_op jit(solution)/shard_map/psum | solution.py:254
  440.6 0.6 copy-start.16
  441.3 1145.6 %all-reduce.6.cloned.1.call-start = ((), (), s32[]{:S(2)}) async-start(), calls=%async_computation.2 | async-start | bytes 139264 | tf_op jit(solution)/shard_map/psum | solution.py:44
Sparse Core Ops, SparseCore 0:
  441.4 1089.3 all-reduce.3
  1533.4 53.4 all-reduce.5
where the time goes:
time: 1630 us; the launch traced here: 1600 us
  waiting for transfers between devices  1390 us (85%)
  matrix products  83 us (5%)
  other arithmetic  42.7 us (3%)
  local copies, waits for them, and re-layouts  39.7 us (2%)
  starting transfers between devices  20.9 us (1%)
  between operations  17.8 us (1%)
    psum x1, waiting for transfers between devices, on_device(): group_delta = lax.psum(weight_delta, ('gx', 'gy'))  1090 us
    all_to_all x1, waiting for transfers between devices, on_device(): lax.all_to_all(outgoing, ('grp', 'gx', 'gy'), split_axis=0, concat_axis=0...  244 us
    psum x1, waiting for transfers between devices, spread(): return lax.psum(block, axis)  49.1 us
    dot_general x4, matrix products, viscosity_block(): jnp.dot(closure_in, columns, precision=highest) + closure_bias[:, None]  46.1 us
    dot_general x4, matrix products, viscosity_block(): jnp.dot(closure_out, hidden, precision=highest)  36.9 us
  transfers between devices with their start and end apart: 7, of which 5 were waited for; matrix products, arithmetic and copies ran while one was open for 1% of the time, Pallas kernels for 0%

commit v1 on v0

v1 whole, which is shorter than its diff:
```python
import functools

import jax
import jax.numpy as jnp
from jax import lax
from jax.experimental import pallas as pl
from jax.experimental.pallas import tpu as pltpu
from jax.sharding import PartitionSpec as P

F = 5
CH = 64
SUB = 16
CX = 16
CY = 32
CZ = 384
TCAP = 6
INNER = 3
CELLS = 4096
NPARAM = 17280
FIRST = CH * 27 * F
KROWS = 240
BASE = 256
WIDE = CELLS + 2 * BASE
CHUNK = 512

time_step = 0.1
base_viscosity = 0.02
viscosity_gain = 0.2
buoyancy = 0.5
inner_rate = 0.02
outer_rate = 0.01
momentum_decay = 0.9
norm_epsilon = 1e-06
f32 = jnp.float32
bf16 = jnp.bfloat16
NT = (((1,), (1,)), ((), ()))


def iota(shape, dim):
    return lax.broadcasted_iota(jnp.int32, shape, dim)


def closure_table(closure_in, closure_bias):
    half = 0.5 * closure_in
    high = lax.reduce_precision(half, 8, 7)
    low = half - high
    bias = 0.5 * closure_bias
    bias_terms = []
    for _ in range(3):
        term = lax.reduce_precision(bias, 8, 7)
        bias_terms.append(term[:, None])
        bias = bias - term
    high = jnp.repeat(high, 16, axis=1)
    low = jnp.repeat(low, 16, axis=1)
    return jnp.concatenate([high, high, low] + bias_terms + [jnp.zeros((CH, 13), f32)], axis=1).astype(bf16)


def spread_closure(table_ref, wide_ref):
    for part in range(8):
        pick = (iota((128, CH), 0) // 16 + part * 8 == iota((128, CH), 1)).astype(f32).astype(bf16)
        rows = jnp.dot(pick, table_ref[...], preferred_element_type=f32)
        row = iota((128, 256), 0) % 16
        column = iota((128, 256), 1)
        keep = (row == column % 16) | (column >= 240)
        wide_ref[part * 128 : (part + 1) * 128, :] = jnp.where(keep, rows, 0.0).astype(bf16)


def closure(cells, wide_ref, out_ref):
    length = cells.shape[1]
    high = cells.astype(bf16)
    low = (cells - high.astype(f32)).astype(bf16)
    stack = jnp.concatenate([high, low, high, jnp.ones((16, length), bf16)], axis=0)
    total = jnp.zeros((16, length), f32)
    for part in range(8):
        half = jnp.dot(wide_ref[part * 128 : (part + 1) * 128, :], stack, preferred_element_type=f32)
        bent = jnp.tanh(half)
        for k in range(8):
            h = half[k * 16 : (k + 1) * 16]
            t = bent[k * 16 : (k + 1) * 16]
            total = total + out_ref[part * 8 + k] * (h + h * t)
    return viscosity_gain * (jnp.maximum(total, 0.0) + jnp.log1p(jnp.exp(-jnp.abs(total))))


def advance(center, east, west, north, south, upper, lower, eddy):
    viscosity = base_viscosity + eddy
    result = []
    for f in range(F):
        laplacian = east[f] + west[f] + north[f] + south[f] + upper[f] + lower[f] - 6.0 * center[f]
        advection = (
            center[0] * (east[f] - west[f])
            + center[1] * (north[f] - south[f])
            + center[2] * (upper[f] - lower[f])
        )
        value = viscosity * laplacian - 0.5 * advection
        if f == 2:
            value = value + buoyancy * center[3]
        result.append(value)
    return result


def cube_kernel(
    where_ref, out_ref, brick, x_low, x_high, y_low, y_high, table_ref, payload, wide_ref, window, north_rows, south_rows
):
    spread_closure(table_ref, wide_ref)
    y_half = where_ref[0]
    z_block = where_ref[1]
    y_start = pl.multiple_of(y_half * 16, 16)
    turn = lax.rem(CZ + 1 - z_block * 16, CZ)

    def cut(rows):
        rolled = pltpu.roll(rows, turn, 1)[:, :128]
        lane = iota(rolled.shape, 1)
        outside = ((lane == 0) & (z_block == 0)) | ((lane == 17) & (z_block == 23))
        return jnp.where(outside, 0.0, rolled)

    upper_half = y_half == 1
    for f in range(F):
        window[f, 0] = cut(x_low[f, pl.ds(y_start, 16), :])
        window[f, 17] = cut(x_high[f, pl.ds(y_start, 16), :])
        south_rows[f] = cut(jnp.where(upper_half, brick[f, :, 15, :], y_low[f]))
        north_rows[f] = cut(jnp.where(upper_half, y_high[f], brick[f, :, 16, :]))

    def load(x, carry):
        for f in range(F):
            window[f, x + 1] = cut(brick[f, x, pl.ds(y_start, 16), :])
        return carry

    lax.fori_loop(0, CX, load, 0, unroll=2)

    lane = iota((128, 256), 0)
    place = iota((128, 256), 1)
    unfold = (lane - 1 == place % 16).astype(f32).astype(bf16)
    own_row = iota((160, 256), 0) % 16 == iota((160, 256), 1) // 16
    group = iota((16, 160), 1) // 16
    gather = (jnp.where(group < 5, group, group + 3) == iota((16, 160), 0)).astype(f32).astype(bf16)
    row = iota((16, 128), 0)

    def quarter(i, carry):
        x0 = i * 4
        cells = jnp.concatenate(
            [
                jnp.concatenate([window[f, x0 + j + 1] for f in range(F)], axis=0)
                for j in range(4)
            ],
            axis=1,
        )
        eddies = closure(cells, wide_ref, out_ref)
        for j in range(4):
            x = x0 + j
            center = [window[f, x + 1] for f in range(F)]
            east = [window[f, x + 2] for f in range(F)]
            west = [window[f, x] for f in range(F)]
            north = [
                jnp.where(row == 15, north_rows[f, pl.ds(x, 1), :], pltpu.roll(center[f], 15, 0)) for f in range(F)
            ]
            south = [
                jnp.where(row == 0, south_rows[f, pl.ds(x, 1), :], pltpu.roll(center[f], 1, 0)) for f in range(F)
            ]
            upper = [pltpu.roll(center[f], 127, 1) for f in range(F)]
            lower = [pltpu.roll(center[f], 1, 1) for f in range(F)]
            tendency = advance(
                center, east, west, north, south, upper, lower, eddies[:, j * 128 : (j + 1) * 128]
            )
            both = jnp.concatenate(center + tendency, axis=0).astype(bf16)
            flat = jnp.dot(both, unfold, preferred_element_type=f32)
            flat = jnp.where(own_row, flat, 0.0).astype(bf16)
            flat = jnp.dot(gather, flat, preferred_element_type=f32).astype(bf16)
            payload[:, pl.ds(pl.multiple_of(x * 256, 256), 256)] = flat
        return carry

    lax.fori_loop(0, 4, quarter, 0)


def cube_call(where, closure_out, brick, x_low, x_high, y_low, y_high, table):
    smem = pl.BlockSpec(memory_space=pltpu.SMEM)
    vmem = pl.BlockSpec(memory_space=pltpu.VMEM)
    return pl.pallas_call(
        cube_kernel,
        out_shape=jax.ShapeDtypeStruct((16, CELLS), bf16),
        in_specs=[smem, smem] + [vmem] * 6,
        out_specs=vmem,
        scratch_shapes=[
            pltpu.VMEM((1024, 256), bf16),
            pltpu.VMEM((F, 18, 16, 128), f32),
            pltpu.VMEM((F, 16, 128), f32),
            pltpu.VMEM((F, 16, 128), f32),
        ],
        compiler_params=pltpu.CompilerParams(vmem_limit_bytes=40 * 2**20),
    )(where, closure_out, brick, x_low, x_high, y_low, y_high, table)


def evolve(out_ref, brick, x_low, x_high, y_low, y_high, table_ref, new_fields, wide_ref, padded, fresh, sems):
    copies = [
        pltpu.make_async_copy(brick, padded.at[:, pl.ds(1, CX)], sems.at[0]),
        pltpu.make_async_copy(x_low, padded.at[:, 0], sems.at[1]),
        pltpu.make_async_copy(x_high, padded.at[:, CX + 1], sems.at[2]),
    ]
    for copy in copies:
        copy.start()
    spread_closure(table_ref, wide_ref)
    for copy in copies:
        copy.wait()
    row = iota((CY, CZ), 0)
    lane = iota((CY, CZ), 1)

    def plane(x, carry):
        center = [padded[f, x + 1] for f in range(F)]
        cells = jnp.concatenate(
            [jnp.concatenate([c[h * 16 : (h + 1) * 16] for c in center], axis=0) for h in range(2)], axis=1
        )
        eddy = closure(cells, wide_ref, out_ref)
        eddy = jnp.concatenate([eddy[:, :CZ], eddy[:, CZ:]], axis=0)
        center = [padded[f, x + 1] for f in range(F)]
        east = [padded[f, x + 2] for f in range(F)]
        west = [padded[f, x] for f in range(F)]
        north = [
            jnp.where(row == CY - 1, y_high[f, pl.ds(x, 1), :], pltpu.roll(center[f], CY - 1, 0)) for f in range(F)
        ]
        south = [jnp.where(row == 0, y_low[f, pl.ds(x, 1), :], pltpu.roll(center[f], 1, 0)) for f in range(F)]
        upper = [jnp.where(lane == CZ - 1, 0.0, pltpu.roll(center[f], CZ - 1, 1)) for f in range(F)]
        lower = [jnp.where(lane == 0, 0.0, pltpu.roll(center[f], 1, 1)) for f in range(F)]
        tendency = advance(center, east, west, north, south, upper, lower, eddy)
        for f in range(F):
            fresh[f, x] = center[f] + time_step * tendency[f]
        pltpu.make_async_copy(fresh.at[:, x], new_fields.at[:, x], sems.at[3]).start()
        return carry

    lax.fori_loop(0, CX, plane, 0)
    pltpu.make_async_copy(fresh, new_fields, sems.at[3]).wait()


def shifted(values, y_step, z_step):
    length = values.shape[1]
    offset = 16 * y_step + z_step
    place = iota(values.shape, 1)
    if y_step:
        y = place // 16 % 16 + y_step
        inside = (y >= 0) & (y < 16)
    else:
        z = place % 16 + z_step
        inside = (z >= 0) & (z < 16)
    return jnp.where(inside, pltpu.roll(values, -offset % length, 1), 0.0)


STEPS = (-1, 0, 1)


def nine(values, sign):
    along_z = {s: values if s == 0 else shifted(values, 0, sign * s) for s in STEPS}
    rows = []
    for y_step in STEPS:
        for z_step in STEPS:
            part = along_z[z_step]
            rows.append(part if y_step == 0 else shifted(part, sign * y_step, 0))
    rows.append(jnp.zeros_like(values))
    return jnp.concatenate(rows, axis=0)


def train(scale_ref, cubes, start, delta, stacks, hiddens, slopes, errors, pres, now_first, now_last, now_out, grads):
    chunks = CELLS // CHUNK
    for x_step in STEPS:
        edge = slice(BASE, 2 * BASE) if x_step < 0 else slice(CELLS, CELLS + BASE)
        if x_step:
            block = x_step + 1
            empty = slice(BASE, 2 * BASE) if x_step > 0 else slice(CELLS, CELLS + BASE)
            errors[block * 80 : (block + 1) * 80, empty] = jnp.zeros((80, BASE), bf16)
            hiddens[block * CH : (block + 1) * CH, edge] = jnp.zeros((CH, BASE), bf16)
            for s in range(TCAP):
                stacks[s, block * 80 : (block + 1) * 80, edge] = jnp.zeros((80, BASE), bf16)

    def build(s, carry):
        for i in range(chunks):
            o = i * CHUNK
            values = cubes[s, :, o : o + CHUNK].astype(f32)[:8]
            rows = nine(values, 1).astype(bf16)
            for x_step in STEPS:
                at = BASE + o - BASE * x_step
                stacks[s, (x_step + 1) * 80 : (x_step + 2) * 80, at : at + CHUNK] = rows
        return carry

    lax.fori_loop(0, TCAP, build, 0)
    delta[...] = jnp.zeros_like(delta)
    eye = (iota((KROWS, KROWS), 0) == iota((KROWS, KROWS), 1)).astype(f32).astype(bf16)

    def step(k, carry):
        first = (start[0] - delta[0])[:, :KROWS].astype(bf16)
        last = (start[1] - delta[1])[:, :KROWS].astype(bf16)
        now_first[...] = first
        now_last[...] = last
        turned = lax.dot_general(eye, last, NT, preferred_element_type=f32)
        now_out[...] = jnp.concatenate([turned[b * 80 : (b + 1) * 80] for b in range(3)], axis=1).astype(bf16)
        grads[...] = jnp.zeros_like(grads)

        def cube(s, carry):
            scale = scale_ref[s]
            for i in range(chunks):
                o = BASE + i * CHUNK
                pre = jnp.dot(now_first[...], stacks[s, :, o : o + CHUNK], preferred_element_type=f32)
                sigmoid = 0.5 + 0.5 * jnp.tanh(0.5 * pre)
                hidden = pre * sigmoid
                slopes[:, i * CHUNK : (i + 1) * CHUNK] = sigmoid + hidden * (1.0 - sigmoid)
                hidden = hidden.astype(bf16)
                for x_step in STEPS:
                    at = o - BASE * x_step
                    hiddens[(x_step + 1) * CH : (x_step + 2) * CH, at : at + CHUNK] = hidden
            for i in range(chunks):
                o = BASE + i * CHUNK
                parts = jnp.dot(now_out[...], hiddens[:, o : o + CHUNK], preferred_element_type=f32)
                predicted = None
                for z_step in STEPS:
                    line = None
                    for y_step in STEPS:
                        row = ((y_step + 1) * 3 + z_step + 1) * 8
                        part = parts[row : row + 8]
                        part = part if y_step == 0 else shifted(part, y_step, 0)
                        line = part if line is None else line + part
                    line = line if z_step == 0 else shifted(line, 0, z_step)
                    predicted = line if predicted is None else predicted + line
                targets = cubes[s, :, i * CHUNK : (i + 1) * CHUNK].astype(f32)[8:]
                error = (scale * (predicted - targets)).astype(bf16).astype(f32)
                rows = nine(error, -1).astype(bf16)
                for x_step in STEPS:
                    at = o + BASE * x_step
                    errors[(x_step + 1) * 80 : (x_step + 2) * 80, at : at + CHUNK] = rows
            for i in range(chunks):
                o = BASE + i * CHUNK
                back = jnp.dot(
                    now_last[...], errors[:, o : o + CHUNK], preferred_element_type=f32
                )
                pres[:, i * CHUNK : (i + 1) * CHUNK] = (back * slopes[:, i * CHUNK : (i + 1) * CHUNK]).astype(bf16)
            cells = slice(BASE, BASE + CELLS)
            grads[0] += lax.dot_general(pres[...], stacks[s, :, cells], NT, preferred_element_type=f32)
            grads[1] += lax.dot_general(
                hiddens[CH : 2 * CH, cells], errors[:, cells], NT, preferred_element_type=f32
            )
            return carry

        lax.fori_loop(0, TCAP, cube, 0)
        delta[:, :, :KROWS] += inner_rate * grads[...]
        return carry

    lax.fori_loop(0, INNER, step, 0)


def work_kernel(
    scale_ref, out_ref, cubes, start, table_ref, y_low, y_high, brick, x_low, x_high,
    new_fields, delta,
    wide_ref, padded, fresh, stacks, hiddens, slopes, errors, pres, now_first, now_last, now_out, grads, sems,
):
    is_trainer = lax.axis_index("grp") == lax.axis_size("grp") - 1

    @pl.when(is_trainer)
    def _():
        copy = pltpu.make_async_copy(brick, new_fields, sems.at[0])
        copy.start()
        train(
            scale_ref, cubes, start, delta, stacks, hiddens, slopes, errors, pres, now_first, now_last, now_out, grads
        )
        copy.wait()

    @pl.when(jnp.logical_not(is_trainer))
    def _():
        delta[...] = jnp.zeros_like(delta)
        evolve(out_ref, brick, x_low, x_high, y_low, y_high, table_ref, new_fields, wide_ref, padded, fresh, sems)


def work_call(scale, closure_out, cubes, start, table, y_low, y_high, brick, x_low, x_high):
    smem = pl.BlockSpec(memory_space=pltpu.SMEM)
    vmem = pl.BlockSpec(memory_space=pltpu.VMEM)
    anywhere = pl.BlockSpec(memory_space=pl.ANY)
    return pl.pallas_call(
        work_kernel,
        out_shape=(
            jax.ShapeDtypeStruct((F, CX, CY, CZ), f32),
            jax.ShapeDtypeStruct((2, CH, 256), f32),
        ),
        in_specs=[smem, smem, vmem, vmem, vmem, vmem, vmem, anywhere, anywhere, anywhere],
        out_specs=(anywhere, vmem),
        scratch_shapes=[
            pltpu.VMEM((1024, 256), bf16),
            pltpu.VMEM((F, CX + 2, CY, CZ), f32),
            pltpu.VMEM((F, CX, CY, CZ), f32),
            pltpu.VMEM((TCAP, KROWS, WIDE), bf16),
            pltpu.VMEM((3 * CH, WIDE), bf16),
            pltpu.VMEM((CH, CELLS), f32),
            pltpu.VMEM((KROWS, WIDE), bf16),
            pltpu.VMEM((CH, CELLS), bf16),
            pltpu.VMEM((CH, KROWS), bf16),
            pltpu.VMEM((CH, KROWS), bf16),
            pltpu.VMEM((80, 3 * CH), bf16),
            pltpu.VMEM((2, CH, KROWS), f32),
            pltpu.SemaphoreType.DMA((4,)),
        ],
        compiler_params=pltpu.CompilerParams(vmem_limit_bytes=56 * 2**20),
    )(scale, closure_out, cubes, start, table, y_low, y_high, brick, x_low, x_high)


def to_tables(flat):
    first = flat[:FIRST].reshape(CH, 3, 9, F)
    last = jnp.transpose(flat[FIRST:].reshape(F, 3, 9, CH), (3, 1, 2, 0))
    both = jnp.stack([first, last])
    both = jnp.pad(both, ((0, 0), (0, 0), (0, 0), (0, 1), (0, 3))).reshape(2, CH, KROWS)
    return jnp.pad(both, ((0, 0), (0, 0), (0, 256 - KROWS)))


def from_tables(both):
    both = both[:, :, :KROWS].reshape(2, CH, 3, 10, 8)[:, :, :, :9, :F]
    first = both[0].reshape(FIRST)
    last = jnp.transpose(both[1], (3, 1, 2, 0)).reshape(FIRST)
    return jnp.concatenate([first, last])


def slot_lists(sample_trainer, column):
    owner_ids = jnp.arange(sample_trainer.shape[0], dtype=jnp.int32)
    same_trainer = sample_trainer[:, None] == sample_trainer[None, :]
    earlier = owner_ids[None, :] < owner_ids[:, None]
    rank_all = jnp.sum((same_trainer & earlier).astype(jnp.int32), axis=1)
    mine_mask = sample_trainer == column
    slot_ids = jnp.arange(TCAP, dtype=jnp.int32)
    chosen = mine_mask[None, :] & (rank_all[None, :] == slot_ids[:, None])
    slot_owner = jnp.sum(jnp.where(chosen, owner_ids[None, :], 0), axis=1)
    slot_valid = jnp.any(chosen, axis=1)
    sample_count = jnp.maximum(jnp.sum(mine_mask.astype(jnp.int32)), 1)
    return (slot_owner, slot_valid, sample_count)


def neighbours(face_low, face_high, axis):
    count = lax.axis_size(axis)
    up = [(i, (i + 1) % count) for i in range(count)]
    down = [((i + 1) % count, i) for i in range(count)]
    return lax.ppermute(face_high, axis, up), lax.ppermute(face_low, axis, down)


def on_device(
    fields, closure_in, closure_bias, closure_out, master, momentum, sample_block, sample_trainer
):
    group_count = lax.axis_size("grp")
    y_devices = lax.axis_size("gy")
    trainers = lax.axis_size("gx") * y_devices
    my_group = lax.axis_index("grp")
    my_column = lax.axis_index("gx") * y_devices + lax.axis_index("gy")
    brick = fields[0]
    x_low, x_high = neighbours(brick[:, 0], brick[:, CX - 1], "gx")
    y_low, y_high = neighbours(brick[:, :, 0], brick[:, :, CY - 1], "gy")
    table = closure_table(closure_in, closure_bias)
    start = to_tables(lax.reduce_precision(master, 8, 7))

    sim_group = jnp.minimum(my_group, group_count - 2)
    block_id = sample_block[sim_group * trainers + my_column]
    where = jnp.stack([block_id // 24, block_id % 24])
    payload = cube_call(where, closure_out, brick, x_low, x_high, y_low, y_high, table)
    arrived = lax.all_gather(payload, ("grp", "gx", "gy"))
    slot_owner, slot_valid, sample_count = slot_lists(sample_trainer, my_column)
    cubes = jnp.stack(
        [lax.dynamic_index_in_dim(arrived, slot_owner[s], 0, keepdims=False) for s in range(TCAP)]
    )
    cubes = jnp.where(slot_valid[:, None, None], cubes, jnp.zeros((), bf16))
    scale = 2.0 * jnp.where(slot_valid, 1.0 / (sample_count.astype(f32) * CELLS), 0.0)
    new_fields, delta = work_call(
        scale, closure_out, cubes, start, table, y_low, y_high, brick, x_low, x_high
    )

    total_delta = from_tables(lax.psum(delta, ("grp", "gx", "gy")))
    share_size = NPARAM // (group_count * trainers)
    share_start = (my_group * trainers + my_column) * share_size
    momentum_share = lax.dynamic_slice_in_dim(momentum, share_start, share_size)
    master_share = lax.dynamic_slice_in_dim(master, share_start, share_size)
    inverse = 1.0 / jnp.sqrt(jnp.sum(total_delta * total_delta) / NPARAM + norm_epsilon)
    delta_share = lax.dynamic_slice_in_dim(total_delta, share_start, share_size)
    new_momentum = momentum_decay * momentum_share + delta_share * inverse
    new_master = master_share - outer_rate * new_momentum
    return (new_fields[None], new_master, new_momentum)


def solution(mesh):
    in_specs = (P("grp", None, "gx", "gy", None), P(), P(), P(), P(), P(), P(), P())
    out_specs = (P("grp", None, "gx", "gy", None), P(("grp", "gx", "gy")), P(("grp", "gx", "gy")))
    return jax.shard_map(
        on_device, mesh=mesh, in_specs=in_specs, out_specs=out_specs, check_vma=False
    )
```

time: 1630 us -> 647 us (0.40); the launches traced: 1600 us -> 646 us
  waiting for transfers between devices: 1390 us -> 552 us
  matrix products: 83 us -> 0 us
  other arithmetic: 42.7 us -> 8.54 us
  Pallas kernels: 0 us -> 30.4 us
  local copies, waits for them, and re-layouts: 39.7 us -> 17.7 us
    psum x2 -> x1, waiting for transfers between devices: 1140 us -> 240 us  [on_device(): total_delta = from_tables(lax.psum(delta, ('grp', 'gx', 'gy')))]
    all_gather x0 -> x1, waiting for transfers between devices: none -> 312 us  [on_device(): arrived = lax.all_gather(payload, ('grp', 'gx', 'gy'))]
    all_to_all x1 -> x0, waiting for transfers between devices: 244 us -> none  [on_device(): lax.all_to_all(outgoing, ('grp', 'gx', 'gy'), split_axis=0, concat_axis=0...]
    dot_general x8 -> x0, matrix products: 83 us -> none  [the longest x4 46.1 us: viscosity_block(): jnp.dot(closure_in, columns, precision=highest) + closure_bias[:, None]]
    pallas_call x0 -> x2, Pallas kernels: none -> 30.4 us  [the longest x1 22.2 us: work_call(): pl.pallas_call(work_kernel, out_shape=(jax.ShapeDtypeStruct((F, CX, CY, C...]
    dynamic_update_slice x4 -> x0, local copies, waits for them, and re-layouts: 18.7 us -> none  [eddy_viscosity(): blocks = lax.map(viscosity_block, jnp.arange(block_count, dtype=jnp.int32))]
  transfers between devices with their start and end apart: 7 -> 6, of which waited for: 5 -> 3; matrix products, arithmetic and copies ran while one was open for 1% -> 2% of each run, Pallas kernels for 0% -> 0%
where the time goes in v1:
time: 647 us; the launch traced here: 646 us
  waiting for transfers between devices  552 us (85%)
  Pallas kernels  30.4 us (5%)
  between operations  28.7 us (4%)
  local copies, waits for them, and re-layouts  17.7 us (3%)
  starting transfers between devices  8.64 us (1%)
  other arithmetic  8.54 us (1%)
    all_gather x1, waiting for transfers between devices, on_device(): arrived = lax.all_gather(payload, ('grp', 'gx', 'gy'))  312 us
    psum x1, waiting for transfers between devices, on_device(): total_delta = from_tables(lax.psum(delta, ('grp', 'gx', 'gy')))  240 us
    pallas_call x1, Pallas kernels, work_call(): pl.pallas_call(work_kernel, out_shape=(jax.ShapeDtypeStruct((F, CX, CY, C...  22.2 us
  transfers between devices with their start and end apart: 6, of which 3 were waited for; matrix products, arithmetic and copies ran while one was open for 2% of the time, Pallas kernels for 0%

profile of v1, /device:TPU:1, one launch (start us, length us, event | category | flops | bytes accessed | tf_op | source)
XLA Modules:
  0.0 646.4 jit_solution(6715067033147766531)
XLA Ops:
  7.2 2.4 copy.82
  9.6 2.2 collective-permute-start
  11.8 3.6 collective-permute-start.1
  15.6 1.3 collective-permute-start.2
  16.9 1.5 collective-permute-start.3
  18.4 0.7 fusion.3
  19.1 0.7 fusion.11
  19.8 1.2 dynamic_slice.31
  24.0 2.2 copy-done
  26.2 0.7 copy-done.6
  26.9 8.1 %shard_map.103 = bf16[16,4096]{1,0:T(8,128)(2,1)} custom-call(s32[2]{0:T(128)S(1)} %pad_add_fusion.where_ref, f32[64]{0:T(128)S(1)} %copy-done.6, f32[5,16,32,384]{3,2,1,0:T(8,128)S(1)} %bitcast.46, f32[5,32,384]{2,1,0:T(8,128)S(1)} %collective-permute-done.x_low, f32[5,32,384]{2,1,0:T(8,128)S(1)} %collective-permute-done.1.x_high, ...), custom_call_target="tpu_custom_call" | custom-call | tf_op jit(solution)/shard_map/pallas_call | solution.py:177
  35.1 0.9 convert_reduce_fusion
  36.0 1.3 convert_reduce_fusion.1
  37.4 0.6 fusion.15
  46.1 0.9 reduce_precision.19
  52.1 0.7 pad.9.start
  52.8 0.5 select_multiply_fusion.scale_ref
  53.3 311.8 %all-gather.3.cloned.1.call-done = bf16[2048,4096]{1,0:T(8,128)(2,1)} async-done(((bf16[16,4096]{1,0:T(8,128)(2,1)}), bf16[2048,4096]{1,0:T(8,128)(2,1)}) %all-gather.3.cloned.1.call-update) | async-done | bytes 16777232 | tf_op jit(solution)/shard_map/all_gather | solution.py:452
  365.2 0.9 dynamic-slice_dynamic-update-slice_fusion.5
  366.1 0.9 dynamic-slice_dynamic-update-slice_fusion.4
  367.0 0.9 dynamic-slice_dynamic-update-slice_fusion.3
  367.9 0.9 dynamic-slice_dynamic-update-slice_fusion.2
  368.9 0.9 dynamic-slice_dynamic-update-slice_fusion.1
  369.8 0.9 dynamic-slice_dynamic-update-slice_fusion
  370.7 1.0 broadcast_select_fusion.cubes
  371.7 22.2 %shard_map.104 = (f32[5,16,32,384]{3,2,1,0:T(8,128)}, f32[2,64,256]{2,1,0:T(8,128)}) custom-call(f32[6]{0:T(128)} %select_multiply_fusion.scale_ref, f32[64]{0:T(128)} %out_ref.3, bf16[6,16,4096]{2,1,0:T(8,128)(2,1)} %broadcast_select_fusion.cubes, f32[2,64,256]{2,1,0:T(8,128)} %pad.9.start, bf16[64,256]{1,0:T(8,128)(2,1)} %copy-done.5, ...), custom_call_target="tpu_custom_call" | custom-call | tf_op jit(solution)/shard_map/pallas_call | solution.py:371
  394.0 240.4 %all-reduce.4.cloned.1.call-done = f32[2,64,256]{2,1,0:T(8,128)} async-done(((f32[2,64,256]{2,1,0:T(8,128)}), f32[2,64,256]{2,1,0:T(8,128)}) %all-reduce.4.cloned.1.call-update) | async-done | bytes 131088 | tf_op jit(solution)/shard_map/psum | solution.py:463
  634.4 1.0 copy.73
  635.6 0.7 copy.74
  636.3 0.5 reshape_squeeze.3
  636.9 0.7 fusion.1
  638.2 1.4 multiply_subtract_fusion
  (46 shorter events, 2.9 us)
Async XLA Ops:
  7.2 358.0 %all-gather.3.cloned.1.call-start = ((), (), s32[]{:S(2)}) async-start(), calls=%async_computation.1 | async-start | bytes 16908288 | tf_op jit(solution)/shard_map/all_gather | solution.py:452
  9.6 14.1 %collective-permute-start = (f32[5,32,384]{2,1,0:T(8,128)S(1)}, f32[5,32,384]{2,1,0:T(8,128)S(1)}, u32[]{:S(2)}, u32[]{:S(2)}) collective-permute-start(f32[5,32,384]{2,1,0:T(8,128)S(1)} %get-tuple-element.14), channel_id=1, source_target_pairs={{0,4},{4,8},{8,12},{12,16},{16,20},{20,24},{24,28},{28,0},{1,5},{5... | collective-permute-start | bytes 737288 | tf_op jit(solution)/shard_map/ppermute | solution.py:431
  11.8 12.1 %collective-permute-start.1 = (f32[5,32,384]{2,1,0:T(8,128)S(1)}, f32[5,32,384]{2,1,0:T(8,128)S(1)}, u32[]{:S(2)}, u32[]{:S(2)}) collective-permute-start(f32[5,32,384]{2,1,0:T(8,128)S(1)} %get-tuple-element.13), channel_id=1, source_target_pairs={{4,0},{8,4},{12,8},{16,12},{20,16},{24,20},{28,24},{0,28},{5,1},{9... | collective-permute-start | bytes 737288 | tf_op jit(solution)/shard_map/ppermute | solution.py:431
  15.6 8.2 %collective-permute-start.2 = (f32[5,16,384]{2,1,0:T(8,128)S(1)}, f32[5,16,384]{2,1,0:T(8,128)S(1)}, u32[]{:S(2)}, u32[]{:S(2)}) collective-permute-start(f32[5,16,384]{2,1,0:T(8,128)S(1)} %bitcast.53), channel_id=1, source_target_pairs={{0,1},{1,2},{2,3},{3,0},{4,5},{5,6},{6,7},{7,4},{8,9},{9,10},{10,1... | collective-permute-start | bytes 368648 | tf_op jit(solution)/shard_map/ppermute | solution.py:431
  16.9 6.9 %collective-permute-start.3 = (f32[5,16,384]{2,1,0:T(8,128)S(1)}, f32[5,16,384]{2,1,0:T(8,128)S(1)}, u32[]{:S(2)}, u32[]{:S(2)}) collective-permute-start(f32[5,16,384]{2,1,0:T(8,128)S(1)} %bitcast.54), channel_id=1, source_target_pairs={{1,0},{2,1},{3,2},{0,3},{5,4},{6,5},{7,6},{4,7},{9,8},{10,9},{11,1... | collective-permute-start | bytes 368648 | tf_op jit(solution)/shard_map/ppermute | solution.py:431
  23.7 348.0 %copy-start.5 = (bf16[64,256]{1,0:T(8,128)(2,1)}, bf16[64,256]{1,0:T(8,128)(2,1)S(1)}, u32[]{:S(2)}) copy-start(bf16[64,256]{1,0:T(8,128)(2,1)S(1)} %concatenate.7.table_ref) | copy-start | bytes 98308
  23.8 347.9 %copy-start.3 = (f32[5,16,384]{2,1,0:T(8,128)}, f32[5,16,384]{2,1,0:T(8,128)S(1)}, u32[]{:S(2)}) copy-start(f32[5,16,384]{2,1,0:T(8,128)S(1)} %collective-permute-done.2.y_low) | copy-start | bytes 368644
  23.8 347.9 %copy-start.4 = (f32[5,16,384]{2,1,0:T(8,128)}, f32[5,16,384]{2,1,0:T(8,128)S(1)}, u32[]{:S(2)}) copy-start(f32[5,16,384]{2,1,0:T(8,128)S(1)} %collective-permute-done.3.y_high) | copy-start | bytes 368644
  23.8 347.9 %copy-start.1 = (f32[5,32,384]{2,1,0:T(8,128)}, f32[5,32,384]{2,1,0:T(8,128)S(1)}, u32[]{:S(2)}) copy-start(f32[5,32,384]{2,1,0:T(8,128)S(1)} %collective-permute-done.x_low) | copy-start | bytes 737284
  24.0 347.7 %copy-start.2 = (f32[5,32,384]{2,1,0:T(8,128)}, f32[5,32,384]{2,1,0:T(8,128)S(1)}, u32[]{:S(2)}) copy-start(f32[5,32,384]{2,1,0:T(8,128)S(1)} %collective-permute-done.1.x_high) | copy-start | bytes 737284
  24.0 2.2 copy-start
  26.2 0.7 copy-start.6
  35.0 599.4 %all-reduce.4.cloned.1.call-start = ((), (), s32[]{:S(2)}) async-start(), calls=%async_computation | async-start | bytes 262144 | tf_op jit(solution)/shard_map/psum | solution.py:463
Sparse Core Ops, SparseCore 0:
  35.1 329.9 all-gather.2
  394.1 240.2 all-reduce.3

commit v2 on v1

v2 whole, which is shorter than its diff:
```python
import jax
import jax.numpy as jnp
from jax import lax
from jax.experimental import pallas as pl
from jax.experimental.pallas import tpu as pltpu
from jax.sharding import PartitionSpec as P

F = 5
CH = 64
SUB = 16
CX = 16
CY = 32
CZ = 384
INNER = 3
CELLS = 4096
NPARAM = 17280
FIRST = CH * 27 * F
OWNERS = 96
TRAINERS = 32
TILES = 32
KROWS = 240
BASE = 256
WIDE = CELLS + 2 * BASE
CHUNK = 512

time_step = 0.1
base_viscosity = 0.02
viscosity_gain = 0.2
buoyancy = 0.5
inner_rate = 0.02
outer_rate = 0.01
momentum_decay = 0.9
norm_epsilon = 1e-06
f32 = jnp.float32
bf16 = jnp.bfloat16
NT = (((1,), (1,)), ((), ()))


def iota(shape, dim):
    return lax.broadcasted_iota(jnp.int32, shape, dim)


def spread_closure(closure_in, closure_bias, wide_ref):
    half = 0.5 * closure_in[...]
    high = half.astype(bf16)
    low = (half - high.astype(f32)).astype(bf16)
    column = iota((F, 256), 1)
    fields = (iota((F, 256), 0) == column // 16 % F) & (column < 240)
    of_high = (fields & (column < 160)).astype(f32).astype(bf16)
    of_low = (fields & (column >= 160)).astype(f32).astype(bf16)
    table = jnp.dot(high, of_high, preferred_element_type=f32) + jnp.dot(low, of_low, preferred_element_type=f32)
    diagonal = iota((CH, CH), 0) == iota((CH, CH), 1)
    bias = 0.5 * jnp.sum(jnp.where(diagonal, closure_bias[...], 0.0), axis=1, keepdims=True)
    lane = iota((CH, 256), 1)
    for place in range(240, 243):
        term = bias.astype(bf16).astype(f32)
        table = jnp.where(lane == place, term, table)
        bias = bias - term
    table = table.astype(bf16)
    for part in range(8):
        pick = (iota((128, CH), 0) // 16 + part * 8 == iota((128, CH), 1)).astype(f32).astype(bf16)
        rows = jnp.dot(pick, table, preferred_element_type=f32)
        row = iota((128, 256), 0) % 16
        column = iota((128, 256), 1)
        keep = (row == column % 16) | (column >= 240)
        wide_ref[part * 128 : (part + 1) * 128, :] = jnp.where(keep, rows, 0.0).astype(bf16)


def closure(cells, wide_ref, out_ref):
    length = cells.shape[1]
    high = cells.astype(bf16)
    low = (cells - high.astype(f32)).astype(bf16)
    stack = jnp.concatenate([high, low, high, jnp.ones((16, length), bf16)], axis=0)
    total = jnp.zeros((16, length), f32)
    for part in range(8):
        half = jnp.dot(wide_ref[part * 128 : (part + 1) * 128, :], stack, preferred_element_type=f32)
        bent = jnp.tanh(half)
        for k in range(8):
            h = half[k * 16 : (k + 1) * 16]
            t = bent[k * 16 : (k + 1) * 16]
            total = total + out_ref[part * 8 + k] * (h + h * t)
    return viscosity_gain * (jnp.maximum(total, 0.0) + jnp.log1p(jnp.exp(-jnp.abs(total))))


def advance(center, east, west, north, south, upper, lower, eddy):
    viscosity = base_viscosity + eddy
    result = []
    for f in range(F):
        laplacian = east[f] + west[f] + north[f] + south[f] + upper[f] + lower[f] - 6.0 * center[f]
        advection = (
            center[0] * (east[f] - west[f])
            + center[1] * (north[f] - south[f])
            + center[2] * (upper[f] - lower[f])
        )
        value = viscosity * laplacian - 0.5 * advection
        if f == 2:
            value = value + buoyancy * center[3]
        result.append(value)
    return result


def cut_cube(block, out_ref, padded, y_low, y_high, payload, wide_ref, window, north_rows, south_rows):
    upper_half = block // 24 == 1
    z_block = block % 24
    turn = lax.rem(CZ + 1 - z_block * 16, CZ)

    def cut(rows):
        rolled = pltpu.roll(rows, turn, 1)[:, :128]
        lane = iota(rolled.shape, 1)
        outside = ((lane == 0) & (z_block == 0)) | ((lane == 17) & (z_block == 23))
        return jnp.where(outside, 0.0, rolled)

    for f in range(F):
        south_rows[f] = cut(jnp.where(upper_half, padded[f, 1 : CX + 1, 15, :], y_low[f]))
        north_rows[f] = cut(jnp.where(upper_half, y_high[f], padded[f, 1 : CX + 1, 16, :]))

    def load(x, carry):
        for f in range(F):
            window[f, x] = cut(jnp.where(upper_half, padded[f, x, 16:, :], padded[f, x, :16, :]))
        return carry

    lax.fori_loop(0, CX + 2, load, 0, unroll=2)

    lane = iota((128, 256), 0)
    place = iota((128, 256), 1)
    unfold = (lane - 1 == place % 16).astype(f32).astype(bf16)
    own_row = iota((160, 256), 0) % 16 == iota((160, 256), 1) // 16
    group = iota((16, 160), 1) // 16
    gather = (jnp.where(group < 5, group, group + 3) == iota((16, 160), 0)).astype(f32).astype(bf16)
    row = iota((16, 128), 0)

    def quarter(i, carry):
        x0 = i * 4
        cells = jnp.concatenate(
            [jnp.concatenate([window[f, x0 + j + 1] for f in range(F)], axis=0) for j in range(4)], axis=1
        )
        eddies = closure(cells, wide_ref, out_ref)
        for j in range(4):
            x = x0 + j
            center = [window[f, x + 1] for f in range(F)]
            east = [window[f, x + 2] for f in range(F)]
            west = [window[f, x] for f in range(F)]
            north = [
                jnp.where(row == 15, north_rows[f, pl.ds(x, 1), :], pltpu.roll(center[f], 15, 0)) for f in range(F)
            ]
            south = [
                jnp.where(row == 0, south_rows[f, pl.ds(x, 1), :], pltpu.roll(center[f], 1, 0)) for f in range(F)
            ]
            upper = [pltpu.roll(center[f], 127, 1) for f in range(F)]
            lower = [pltpu.roll(center[f], 1, 1) for f in range(F)]
            tendency = advance(
                center, east, west, north, south, upper, lower, eddies[:, j * 128 : (j + 1) * 128]
            )
            both = jnp.concatenate(center + tendency, axis=0).astype(bf16)
            flat = jnp.dot(both, unfold, preferred_element_type=f32)
            flat = jnp.where(own_row, flat, 0.0).astype(bf16)
            flat = jnp.dot(gather, flat, preferred_element_type=f32).astype(bf16)
            payload[:, pl.ds(pl.multiple_of(x * 256, 256), 256)] = flat
        return carry

    lax.fori_loop(0, 4, quarter, 0)


def evolve(begin, end, out_ref, padded, y_low, y_high, new_fields, wide_ref, fresh, sem):
    row = iota((CY, CZ), 0)
    lane = iota((CY, CZ), 1)

    def plane(x, carry):
        center = [padded[f, x + 1] for f in range(F)]
        cells = jnp.concatenate(
            [jnp.concatenate([c[h * 16 : (h + 1) * 16] for c in center], axis=0) for h in range(2)], axis=1
        )
        eddy = closure(cells, wide_ref, out_ref)
        eddy = jnp.concatenate([eddy[:, :CZ], eddy[:, CZ:]], axis=0)
        center = [padded[f, x + 1] for f in range(F)]
        east = [padded[f, x + 2] for f in range(F)]
        west = [padded[f, x] for f in range(F)]
        north = [
            jnp.where(row == CY - 1, y_high[f, pl.ds(x, 1), :], pltpu.roll(center[f], CY - 1, 0)) for f in range(F)
        ]
        south = [jnp.where(row == 0, y_low[f, pl.ds(x, 1), :], pltpu.roll(center[f], 1, 0)) for f in range(F)]
        upper = [jnp.where(lane == CZ - 1, 0.0, pltpu.roll(center[f], CZ - 1, 1)) for f in range(F)]
        lower = [jnp.where(lane == 0, 0.0, pltpu.roll(center[f], 1, 1)) for f in range(F)]
        tendency = advance(center, east, west, north, south, upper, lower, eddy)
        for f in range(F):
            fresh[f, x] = center[f] + time_step * tendency[f]
        return carry

    lax.fori_loop(begin, end, plane, 0)
    copy = pltpu.make_async_copy(
        fresh.at[:, pl.ds(begin, end - begin)], new_fields.at[:, pl.ds(begin, end - begin)], sem
    )
    copy.start()
    return copy


def shifted(values, y_step, z_step):
    length = values.shape[1]
    offset = 16 * y_step + z_step
    place = iota(values.shape, 1)
    if y_step:
        y = place // 16 % 16 + y_step
        inside = (y >= 0) & (y < 16)
    else:
        z = place % 16 + z_step
        inside = (z >= 0) & (z < 16)
    return jnp.where(inside, pltpu.roll(values, -offset % length, 1), 0.0)


STEPS = (-1, 0, 1)


def nine(values, sign):
    along_z = {s: values if s == 0 else shifted(values, 0, sign * s) for s in STEPS}
    rows = []
    for y_step in STEPS:
        for z_step in STEPS:
            part = along_z[z_step]
            rows.append(part if y_step == 0 else shifted(part, sign * y_step, 0))
    rows.append(jnp.zeros_like(values))
    return jnp.concatenate(rows, axis=0)


def build_stack(payload, stack, hiddens, errors):
    for x_step in STEPS:
        if x_step:
            block = x_step + 1
            ends = (slice(BASE, 2 * BASE), slice(CELLS, CELLS + BASE))
            edge, empty = ends if x_step < 0 else ends[::-1]
            errors[block * 80 : (block + 1) * 80, empty] = jnp.zeros((80, BASE), bf16)
            hiddens[block * CH : (block + 1) * CH, edge] = jnp.zeros((CH, BASE), bf16)
            stack[block * 80 : (block + 1) * 80, edge] = jnp.zeros((80, BASE), bf16)
    for o in range(0, CELLS, CHUNK):
        rows = nine(payload[:, o : o + CHUNK].astype(f32)[:8], 1).astype(bf16)
        for x_step in STEPS:
            at = BASE + o - BASE * x_step
            stack[(x_step + 1) * 80 : (x_step + 2) * 80, at : at + CHUNK] = rows


def table_of(tiles, layer):
    return jnp.concatenate(
        [tiles[layer * 128 : layer * 128 + 64, :], tiles[layer * 128 + 64 : layer * 128 + 128, :]], axis=1
    )


def set_table(tiles, layer, table):
    tiles[layer * 128 : layer * 128 + 64, :] = table[:, :128]
    tiles[layer * 128 + 64 : layer * 128 + 128, :] = table[:, 128:]


def gradient(scale, weights, payload, stack, hiddens, slopes, errors, pres, now_first, now_last, now_out, grad):
    eye = (iota((KROWS, KROWS), 0) == iota((KROWS, KROWS), 1)).astype(f32).astype(bf16)
    now_first[...] = table_of(weights, 0)[:, :KROWS].astype(bf16)
    last = table_of(weights, 1)[:, :KROWS].astype(bf16)
    now_last[...] = last
    turned = lax.dot_general(eye, last, NT, preferred_element_type=f32)
    now_out[...] = jnp.concatenate([turned[b * 80 : (b + 1) * 80] for b in range(3)], axis=1).astype(bf16)
    for i in range(0, CELLS, CHUNK):
        o = BASE + i
        pre = jnp.dot(now_first[...], stack[:, o : o + CHUNK], preferred_element_type=f32)
        sigmoid = 0.5 + 0.5 * jnp.tanh(0.5 * pre)
        hidden = pre * sigmoid
        slopes[:, i : i + CHUNK] = sigmoid + hidden * (1.0 - sigmoid)
        hidden = hidden.astype(bf16)
        for x_step in STEPS:
            at = o - BASE * x_step
            hiddens[(x_step + 1) * CH : (x_step + 2) * CH, at : at + CHUNK] = hidden
    for i in range(0, CELLS, CHUNK):
        o = BASE + i
        parts = jnp.dot(now_out[...], hiddens[:, o : o + CHUNK], preferred_element_type=f32)
        predicted = None
        for z_step in STEPS:
            line = None
            for y_step in STEPS:
                row = ((y_step + 1) * 3 + z_step + 1) * 8
                part = parts[row : row + 8]
                part = part if y_step == 0 else shifted(part, y_step, 0)
                line = part if line is None else line + part
            line = line if z_step == 0 else shifted(line, 0, z_step)
            predicted = line if predicted is None else predicted + line
        targets = payload[:, i : i + CHUNK].astype(f32)[8:]
        error = (scale * (predicted - targets)).astype(bf16).astype(f32)
        rows = nine(error, -1).astype(bf16)
        for x_step in STEPS:
            at = o + BASE * x_step
            errors[(x_step + 1) * 80 : (x_step + 2) * 80, at : at + CHUNK] = rows
    for i in range(0, CELLS, CHUNK):
        o = BASE + i
        back = jnp.dot(now_last[...], errors[:, o : o + CHUNK], preferred_element_type=f32)
        pres[:, i : i + CHUNK] = (back * slopes[:, i : i + CHUNK]).astype(bf16)
    cells = slice(BASE, BASE + CELLS)
    spare = jnp.zeros((CH, 256 - KROWS), f32)
    first = lax.dot_general(pres[...], stack[:, cells], NT, preferred_element_type=f32)
    set_table(grad, 0, jnp.concatenate([first, spare], axis=1))
    last = lax.dot_general(hiddens[CH : 2 * CH, cells], errors[:, cells], NT, preferred_element_type=f32)
    set_table(grad, 1, jnp.concatenate([last, spare], axis=1))


def three_terms(values):
    high = values.astype(bf16)
    rest = values - high.astype(f32)
    middle = rest.astype(bf16)
    return high, middle, (rest - middle.astype(f32)).astype(bf16)


def places(layer):
    lane = iota((135, 256), 1)
    x_step, rest = lane // 80, lane % 80
    offset, field = x_step * 9 + rest // 8, rest % 8
    index = offset * F + field if layer == 0 else field * 27 + offset
    valid = (lane < KROWS) & (rest < 72) & (field < F)
    return (valid & (index == iota((135, 256), 0))).astype(f32).astype(bf16)


def device(group, column):
    columns = lax.axis_size("gy")
    return {"grp": group, "gx": column // columns, "gy": lax.rem(column, columns)}


def whole(ref, sem):
    return pltpu.make_async_copy(ref, ref, sem)


def step_kernel(
    block_ref, trainer_ref, out_ref, closure_in, closure_bias, trainer_row, first_in, last_in, brick,
    new_fields, first_out, last_out,
    wide_ref, padded, fresh, y_low, y_high, y_send, payload, window, north_rows, south_rows,
    stack, hiddens, slopes, errors, pres, now_first, now_last, now_out,
    start, weights, grad, gathered, answer, running, delta,
    load_sem, halo_send, halo_recv, store_sems, up_send, up_recv, down_send, down_recv, last_send, last_recv,
):
    group = lax.axis_index("grp")
    column = lax.axis_index("gx") * lax.axis_size("gy") + lax.axis_index("gy")
    me = group * TRAINERS + column
    last_group = lax.axis_size("grp") - 1

    def start_tables():
        table = jnp.dot(first_in[...].astype(bf16), places(0), preferred_element_type=f32)
        set_table(start, 0, table)
        table = lax.dot_general(
            last_in[...].astype(bf16), places(1), (((0,), (0,)), ((), ())), preferred_element_type=f32
        )
        set_table(start, 1, table)

    @pl.when(group < last_group)
    def _():
        load = pltpu.make_async_copy(brick, padded.at[:, pl.ds(1, CX)], load_sem)
        load.start()
        gx, gy = lax.axis_index("gx"), lax.axis_index("gy")
        gx_size, gy_size = lax.axis_size("gx"), lax.axis_size("gy")
        x_next, x_last = lax.rem(gx + 1, gx_size), lax.rem(gx + gx_size - 1, gx_size)
        y_next, y_last = lax.rem(gy + 1, gy_size), lax.rem(gy + gy_size - 1, gy_size)
        to_next_x = pltpu.make_async_remote_copy(
            brick.at[:, CX - 1], padded.at[:, 0], halo_send.at[0], halo_recv.at[0], device_id={"gx": x_next}
        )
        to_last_x = pltpu.make_async_remote_copy(
            brick.at[:, 0], padded.at[:, CX + 1], halo_send.at[1], halo_recv.at[1], device_id={"gx": x_last}
        )
        to_next_x.start()
        to_last_x.start()
        load.wait()
        for f in range(F):
            y_send[0, f] = padded[f, 1 : CX + 1, CY - 1, :]
            y_send[1, f] = padded[f, 1 : CX + 1, 0, :]
        to_next_y = pltpu.make_async_remote_copy(
            y_send.at[0], y_low, halo_send.at[2], halo_recv.at[2], device_id={"gy": y_next}
        )
        to_last_y = pltpu.make_async_remote_copy(
            y_send.at[1], y_high, halo_send.at[3], halo_recv.at[3], device_id={"gy": y_last}
        )
        to_next_y.start()
        to_last_y.start()
        spread_closure(closure_in, closure_bias, wide_ref)
        start_tables()
        same = (trainer_row[...] == trainer_ref[me]).astype(f32)
        count = jnp.sum(same, axis=1, keepdims=True)
        scale = 2.0 * (1.0 / (count * CELLS))
        for copy in (to_next_x, to_last_x, to_next_y, to_last_y):
            copy.wait()
        cut_cube(block_ref[me], out_ref, padded, y_low, y_high, payload, wide_ref, window, north_rows, south_rows)
        build_stack(payload, stack, hiddens, errors)
        bounds = (0, 5, 10, CX)
        stores = []
        for k in range(INNER):
            gradient(
                scale, weights if k else start, payload, stack, hiddens, slopes, errors, pres,
                now_first, now_last, now_out, grad,
            )

            def send(j, carry):
                to = lax.rem(column + j, TILES)
                pltpu.make_async_remote_copy(
                    grad.at[pl.ds(pl.multiple_of(to * 8, 8), 8)],
                    gathered.at[pl.ds(pl.multiple_of(me * 8, 8), 8)],
                    up_send,
                    up_recv,
                    device_id=device(last_group, to),
                ).start()
                return carry

            lax.fori_loop(0, TILES, send, 0, unroll=4)
            stores.append(
                evolve(
                    bounds[k], bounds[k + 1], out_ref, padded, y_low, y_high, new_fields, wide_ref, fresh,
                    store_sems.at[k],
                )
            )
            whole(grad, up_send).wait()
            if k < INNER - 1:
                whole(weights, down_recv).wait()
        for store in stores:
            store.wait()
        whole(delta, last_recv).wait()

    @pl.when(group == last_group)
    def _():
        keep = pltpu.make_async_copy(brick, new_fields, load_sem)
        keep.start()
        start_tables()
        own_start = start[pl.ds(pl.multiple_of(column * 8, 8), 8), :]
        square = (OWNERS, OWNERS)
        across = jnp.broadcast_to(trainer_row[...].astype(f32), square)
        diagonal = jnp.where(iota(square, 0) == iota(square, 1), across, 0.0)
        down = jnp.sum(diagonal, axis=1, keepdims=True)
        same = (across == down).astype(f32).astype(bf16)
        running[...] = jnp.zeros_like(running)
        total = jnp.zeros((8, 128), f32)
        for k in range(INNER):
            whole(gathered, up_recv).wait()

            def add(o, total):
                return total + gathered[pl.ds(pl.multiple_of(o * 8, 8), 8), :]

            total = lax.fori_loop(0, OWNERS, add, total, unroll=8)
            if k < INNER - 1:
                if k:
                    whole(answer, down_send).wait()
                for r in range(8):
                    terms = three_terms(gathered[pl.ds(r, OWNERS, stride=8), :])
                    part = sum(jnp.dot(same, term, preferred_element_type=f32) for term in terms)
                    part = running[r] + part
                    running[r] = part
                    answer[pl.ds(r, OWNERS, stride=8), :] = own_start[r : r + 1] - inner_rate * part

                def send(j, carry):
                    to = lax.rem(column + j, TRAINERS)
                    for g in range(OWNERS // TRAINERS):
                        pltpu.make_async_remote_copy(
                            answer.at[pl.ds(pl.multiple_of((g * TRAINERS + to) * 8, 8), 8)],
                            weights.at[pl.ds(pl.multiple_of(column * 8, 8), 8)],
                            down_send,
                            down_recv,
                            device_id=device(g, to),
                        ).start()
                    return carry

                lax.fori_loop(0, TRAINERS, send, 0, unroll=2)
        whole(answer, down_send).wait()
        own = delta.at[pl.ds(pl.multiple_of(column * 8, 8), 8)]
        own[...] = inner_rate * total

        def tell(j, carry):
            to = lax.rem(me + j, OWNERS + TRAINERS)
            pltpu.make_async_remote_copy(
                own, own, last_send, last_recv, device_id=device(to // TRAINERS, lax.rem(to, TRAINERS))
            ).start()
            return carry

        lax.fori_loop(1, OWNERS + TRAINERS, tell, 0)
        others = delta.at[pl.ds(0, (TILES - 1) * 8)]
        whole(others, last_recv).wait()
        for part in range(3):
            whole(delta, last_send).wait()
        whole(others, last_send).wait()
        keep.wait()

    values = delta[...]
    inverse = lax.rsqrt(jnp.sum(values * values) / NPARAM + norm_epsilon)
    first_out[...] = sum(
        lax.dot_general(term, places(0), NT, preferred_element_type=f32)
        for term in three_terms(table_of(delta, 0) * inverse)
    )
    last_out[...] = sum(
        lax.dot_general(places(1), term, NT, preferred_element_type=f32)
        for term in three_terms(table_of(delta, 1) * inverse)
    )


def step_call(sample_block, sample_trainer, closure_out, closure_in, closure_bias, first_in, last_in, brick):
    smem = pl.BlockSpec(memory_space=pltpu.SMEM)
    vmem = pl.BlockSpec(memory_space=pltpu.VMEM)
    anywhere = pl.BlockSpec(memory_space=pl.ANY)
    dma = pltpu.SemaphoreType.DMA
    return pl.pallas_call(
        step_kernel,
        out_shape=(
            jax.ShapeDtypeStruct((F, CX, CY, CZ), f32),
            jax.ShapeDtypeStruct((CH, 135), f32),
            jax.ShapeDtypeStruct((135, CH), f32),
        ),
        in_specs=[smem, smem, smem, vmem, vmem, vmem, vmem, vmem, anywhere],
        out_specs=(anywhere, vmem, vmem),
        scratch_shapes=[
            pltpu.VMEM((1024, 256), bf16),
            pltpu.VMEM((F, CX + 2, CY, CZ), f32),
            pltpu.VMEM((F, CX, CY, CZ), f32),
            pltpu.VMEM((F, CX, CZ), f32),
            pltpu.VMEM((F, CX, CZ), f32),
            pltpu.VMEM((2, F, CX, CZ), f32),
            pltpu.VMEM((16, CELLS), bf16),
            pltpu.VMEM((F, 18, 16, 128), f32),
            pltpu.VMEM((F, 16, 128), f32),
            pltpu.VMEM((F, 16, 128), f32),
            pltpu.VMEM((KROWS, WIDE), bf16),
            pltpu.VMEM((3 * CH, WIDE), bf16),
            pltpu.VMEM((CH, CELLS), f32),
            pltpu.VMEM((KROWS, WIDE), bf16),
            pltpu.VMEM((CH, CELLS), bf16),
            pltpu.VMEM((CH, KROWS), bf16),
            pltpu.VMEM((CH, KROWS), bf16),
            pltpu.VMEM((80, 3 * CH), bf16),
            pltpu.VMEM((TILES * 8, 128), f32),
            pltpu.VMEM((TILES * 8, 128), f32),
            pltpu.VMEM((TILES * 8, 128), f32),
            pltpu.VMEM((OWNERS * 8, 128), f32),
            pltpu.VMEM((OWNERS * 8, 128), f32),
            pltpu.VMEM((8, OWNERS, 128), f32),
            pltpu.VMEM((TILES * 8, 128), f32),
            dma,
            dma((4,)),
            dma((4,)),
            dma((INNER,)),
            dma,
            dma,
            dma,
            dma,
            dma,
            dma,
        ],
        compiler_params=pltpu.CompilerParams(vmem_limit_bytes=48 * 2**20, has_side_effects=True),
    )(
        sample_block, sample_trainer, closure_out, closure_in, closure_bias.reshape(1, CH),
        sample_trainer.reshape(1, OWNERS), first_in, last_in, brick,
    )


def on_device(
    fields, closure_in, closure_bias, closure_out, master, momentum, sample_block, sample_trainer
):
    column = lax.axis_index("gx") * lax.axis_size("gy") + lax.axis_index("gy")
    me = lax.axis_index("grp") * TRAINERS + column
    new_fields, first, last = step_call(
        sample_block,
        sample_trainer,
        closure_out,
        closure_in,
        closure_bias,
        master[:FIRST].reshape(CH, 135),
        master[FIRST:].reshape(135, CH),
        fields[0],
    )
    scaled = jnp.concatenate([first.reshape(FIRST), last.reshape(FIRST)])
    size = NPARAM // (OWNERS + TRAINERS)
    share = [lax.dynamic_slice_in_dim(whole_array, me * size, size) for whole_array in (momentum, master, scaled)]
    new_momentum = momentum_decay * share[0] + share[2]
    new_master = share[1] - outer_rate * new_momentum
    return (new_fields[None], new_master, new_momentum)


def solution(mesh):
    in_specs = (P("grp", None, "gx", "gy", None), P(), P(), P(), P(), P(), P(), P())
    out_specs = (P("grp", None, "gx", "gy", None), P(("grp", "gx", "gy")), P(("grp", "gx", "gy")))
    return jax.shard_map(
        on_device, mesh=mesh, in_specs=in_specs, out_specs=out_specs, check_vma=False
    )
```

time: 647 us -> 95.6 us (0.15)
  waiting for transfers between devices: 552 us -> 0 us
  Pallas kernels: 30.4 us -> 81.9 us
  between operations: 28.7 us -> 0.67 us
  starting transfers between devices: 8.64 us -> 0 us
  other arithmetic: 8.54 us -> 1.38 us
  local copies, waits for them, and re-layouts: 17.7 us -> 11.2 us
    all_gather x1 -> x0, waiting for transfers between devices: 312 us -> none  [on_device(): arrived = lax.all_gather(payload, ('grp', 'gx', 'gy'))]
    psum x1 -> x0, waiting for transfers between devices: 240 us -> none  [on_device(): total_delta = from_tables(lax.psum(delta, ('grp', 'gx', 'gy')))]
    pallas_call x2 -> x1, Pallas kernels: 30.4 us -> 81.9 us  [step_call(): pl.pallas_call(step_kernel, out_shape=(jax.ShapeDtypeStruct((F, CX, CY, C...]
    ppermute x4 -> x0, starting transfers between devices: 8.56 us -> none  [the longest x2 5.09 us: neighbours(): lax.ppermute(face_low, axis, down)]
  transfers between devices with their start and end apart: 6 -> 0, of which waited for: 3 -> 0; matrix products, arithmetic and copies ran while one was open for 2% -> 0% of each run, Pallas kernels for 0% -> 0%
where the time goes in v2:
time: 95.6 us; the launch traced here: 95.2 us
  Pallas kernels  81.9 us (86%)
  local copies, waits for them, and re-layouts  11.2 us (12%)
  other arithmetic  1.38 us (1%)
    pallas_call x1, Pallas kernels, step_call(): pl.pallas_call(step_kernel, out_shape=(jax.ShapeDtypeStruct((F, CX, CY, C...  81.9 us
    unnamed x12, local copies, waits for them, and re-layouts  9.74 us

profile of v2, /device:TPU:1, one launch (start us, length us, event | category | flops | bytes accessed | tf_op | source)
XLA Modules:
  0.0 95.2 jit_solution(1435454008541535468)
XLA Ops:
  0.6 0.9 fusion.1
  1.6 0.1 reshape.40.last_in
  1.6 0.2 slice.25.first_in
  1.8 0.8 copy.12.closure_in
  2.6 0.0 copy-start.1
  2.6 0.7 copy-done.1
  3.3 0.0 copy-start.2
  3.3 0.7 copy-done.2
  3.9 0.0 copy-start.3
  3.9 0.7 copy-done.3
  4.6 0.0 copy-start.4
  4.6 0.7 copy-done.4
  5.2 81.9 %shard_map.103 = (f32[5,16,32,384]{3,2,1,0:T(8,128)S(1)}, f32[64,135]{1,0:T(8,128)S(1)}, f32[135,64]{1,0:T(8,128)S(1)}) custom-call(s32[96]{0:T(128)S(1)} %copy-done.2, s32[96]{0:T(128)S(1)} %copy-done.1, f32[64]{0:T(128)S(1)} %copy-done.3, f32[64,5]{1,0:T(8,128)S(1)} %copy.12.closure_in, f32[1,64]{1,0:T(1,128)S(1)} %bitcast.6, s32[1,96]{1,0:T(1,128)S(1)} %bitcast.5, ...), custom_call_target="tpu_custom_call" | custom-call | tf_op jit(solution)/shard_map/pallas_call | solution.py:494
  87.2 0.0 copy-start
  87.2 1.9 %copy-done = f32[5,16,32,384]{3,2,1,0:T(8,128)} copy-done((f32[5,16,32,384]{3,2,1,0:T(8,128)}, f32[5,16,32,384]{3,2,1,0:T(8,128)S(1)}, u32[]{:S(2)}) %copy-start) | copy-done | bytes 3932184
  89.1 0.2 reshape.41
  89.3 0.1 reshape.42
  89.3 1.4 %multiply_subtract_fusion = (f32[135]{0:T(256)}, f32[135]{0:T(256)}) fusion(f32[17280]{0:T(1024)} %param.12, s32[]{:T(128)S(6)} %select_n.2, f32[8640]{0:T(1024)S(1)} %reshape.42, f32[8640]{0:T(1024)S(1)} %reshape.41, f32[17280]{0:T(1024)} %param.13), kind=kLoop, calls=%fused_computation.3 | loop fusion | flops 675 | bytes 71284 | tf_op jit(solution)/shard_map/sub | solution.py:566
  90.7 4.5 %copy.14 = f32[1,5,16,32,384]{4,3,2,1,0:T(8,128)} copy(f32[1,5,16,32,384]{4,3,2,1,0:T(8,128)} %bitcast.4) | data formatting | bytes 7864320
Async XLA Ops:
  2.6 0.7 copy-start.1
  3.3 0.7 copy-start.2
  3.9 0.7 copy-start.3
  4.6 0.7 copy-start.4
  87.2 1.9 %copy-start = (f32[5,16,32,384]{3,2,1,0:T(8,128)}, f32[5,16,32,384]{3,2,1,0:T(8,128)S(1)}, u32[]{:S(2)}) copy-start(f32[5,16,32,384]{3,2,1,0:T(8,128)S(1)} %get-tuple-element.6) | copy-start | bytes 11796484

commit v3 on v2

--- a/solution.py
+++ b/solution.py
@@ -42,13 +42,15 @@
 
 def spread_closure(closure_in, closure_bias, wide_ref):
     half = 0.5 * closure_in[...]
+    inner = (((0,), (0,)), ((), ()))
     high = half.astype(bf16)
     low = (half - high.astype(f32)).astype(bf16)
     column = iota((F, 256), 1)
     fields = (iota((F, 256), 0) == column // 16 % F) & (column < 240)
     of_high = (fields & (column < 160)).astype(f32).astype(bf16)
     of_low = (fields & (column >= 160)).astype(f32).astype(bf16)
-    table = jnp.dot(high, of_high, preferred_element_type=f32) + jnp.dot(low, of_low, preferred_element_type=f32)
+    table = lax.dot_general(high, of_high, inner, preferred_element_type=f32)
+    table = table + lax.dot_general(low, of_low, inner, preferred_element_type=f32)
     diagonal = iota((CH, CH), 0) == iota((CH, CH), 1)
     bias = 0.5 * jnp.sum(jnp.where(diagonal, closure_bias[...], 0.0), axis=1, keepdims=True)
     lane = iota((CH, 256), 1)
@@ -99,28 +101,45 @@
     return result
 
 
-def cut_cube(block, out_ref, padded, y_low, y_high, payload, wide_ref, window, north_rows, south_rows):
+def cut(rows, z_block):
+    rolled = pltpu.roll(rows, lax.rem(CZ + 1 - z_block * 16, CZ), 1)[:, :128]
+    lane = iota(rolled.shape, 1)
+    outside = ((lane == 0) & (z_block == 0)) | ((lane == 17) & (z_block == 23))
+    return jnp.where(outside, 0.0, rolled)
+
+
+def own_windows(block, out_ref, padded, wide_ref, window, north_rows, south_rows, eddies):
     upper_half = block // 24 == 1
     z_block = block % 24
-    turn = lax.rem(CZ + 1 - z_block * 16, CZ)
-
-    def cut(rows):
-        rolled = pltpu.roll(rows, turn, 1)[:, :128]
-        lane = iota(rolled.shape, 1)
-        outside = ((lane == 0) & (z_block == 0)) | ((lane == 17) & (z_block == 23))
-        return jnp.where(outside, 0.0, rolled)
-
     for f in range(F):
-        south_rows[f] = cut(jnp.where(upper_half, padded[f, 1 : CX + 1, 15, :], y_low[f]))
-        north_rows[f] = cut(jnp.where(upper_half, y_high[f], padded[f, 1 : CX + 1, 16, :]))
+        rows = jnp.where(upper_half, padded[f, 1 : CX + 1, 15, :], padded[f, 1 : CX + 1, 16, :])
+        rows = cut(rows, z_block)
+        south_rows[f] = rows
+        north_rows[f] = rows
 
     def load(x, carry):
         for f in range(F):
-            window[f, x] = cut(jnp.where(upper_half, padded[f, x, 16:, :], padded[f, x, :16, :]))
+            window[f, x] = cut(jnp.where(upper_half, padded[f, x, 16:, :], padded[f, x, :16, :]), z_block)
         return carry
 
-    lax.fori_loop(0, CX + 2, load, 0, unroll=2)
-
+    lax.fori_loop(1, CX + 1, load, 0, unroll=2)
+
+    def quarter(i, carry):
+        x0 = i * 4
+        cells = jnp.concatenate(
+            [jnp.concatenate([window[f, x0 + j + 1] for f in range(F)], axis=0) for j in range(4)], axis=1
+        )
+        eddies[i] = closure(cells, wide_ref, out_ref)
+        return carry
+
+    lax.fori_loop(0, 4, quarter, 0)
+
+
+def cut_cube(block, y_near, payload, window, north_rows, south_rows, eddies):
+    upper_half = block // 24 == 1
+    for f in range(F):
+        south_rows[f] = jnp.where(upper_half, south_rows[f], y_near[0, f])
+        north_rows[f] = jnp.where(upper_half, y_near[1, f], north_rows[f])
     lane = iota((128, 256), 0)
     place = iota((128, 256), 1)
     unfold = (lane - 1 == place % 16).astype(f32).astype(bf16)
@@ -130,13 +149,9 @@
     row = iota((16, 128), 0)
 
     def quarter(i, carry):
-        x0 = i * 4
-        cells = jnp.concatenate(
-            [jnp.concatenate([window[f, x0 + j + 1] for f in range(F)], axis=0) for j in range(4)], axis=1
-        )
-        eddies = closure(cells, wide_ref, out_ref)
+        eddy = eddies[i]
         for j in range(4):
-            x = x0 + j
+            x = i * 4 + j
             center = [window[f, x + 1] for f in range(F)]
             east = [window[f, x + 2] for f in range(F)]
             west = [window[f, x] for f in range(F)]
@@ -149,7 +164,7 @@
             upper = [pltpu.roll(center[f], 127, 1) for f in range(F)]
             lower = [pltpu.roll(center[f], 1, 1) for f in range(F)]
             tendency = advance(
-                center, east, west, north, south, upper, lower, eddies[:, j * 128 : (j + 1) * 128]
+                center, east, west, north, south, upper, lower, eddy[:, j * 128 : (j + 1) * 128]
             )
             both = jnp.concatenate(center + tendency, axis=0).astype(bf16)
             flat = jnp.dot(both, unfold, preferred_element_type=f32)
@@ -161,7 +176,7 @@
     lax.fori_loop(0, 4, quarter, 0)
 
 
-def evolve(begin, end, out_ref, padded, y_low, y_high, new_fields, wide_ref, fresh, sem):
+def evolve(begin, end, out_ref, padded, y_low, y_high, new_fields, wide_ref):
     row = iota((CY, CZ), 0)
     lane = iota((CY, CZ), 1)
 
@@ -183,15 +198,10 @@
         lower = [jnp.where(lane == 0, 0.0, pltpu.roll(center[f], 1, 1)) for f in range(F)]
         tendency = advance(center, east, west, north, south, upper, lower, eddy)
         for f in range(F):
-            fresh[f, x] = center[f] + time_step * tendency[f]
+            new_fields[f, x] = center[f] + time_step * tendency[f]
         return carry
 
     lax.fori_loop(begin, end, plane, 0)
-    copy = pltpu.make_async_copy(
-        fresh.at[:, pl.ds(begin, end - begin)], new_fields.at[:, pl.ds(begin, end - begin)], sem
-    )
-    copy.start()
-    return copy
 
 
 def shifted(values, y_step, z_step):
@@ -303,13 +313,56 @@
     return high, middle, (rest - middle.astype(f32)).astype(bf16)
 
 
-def places(layer):
-    lane = iota((135, 256), 1)
-    x_step, rest = lane // 80, lane % 80
-    offset, field = x_step * 9 + rest // 8, rest % 8
+def lane_of(offset, field):
+    return offset // 9 * 80 + offset % 9 * 8 + field
+
+
+def parameter_of(layer):
+    lane = iota((1, 256), 1)
+    rest = lane % 80
+    offset, field = lane // 80 * 9 + rest // 8, rest % 8
     index = offset * F + field if layer == 0 else field * 27 + offset
-    valid = (lane < KROWS) & (rest < 72) & (field < F)
-    return (valid & (index == iota((135, 256), 0))).astype(f32).astype(bf16)
+    return jnp.where((lane < KROWS) & (rest < 72) & (field < F), index, -1)
+
+
+def one_hot(condition):
+    return condition.astype(f32).astype(bf16)
+
+
+def first_table(flat):
+    wide = jnp.concatenate([flat[m : m + CH] for m in range(5)], axis=1)
+    unit = iota((CH, 640), 0)
+    for bit in range(6):
+        wide = jnp.where(unit // 2**bit % 2 == 1, pltpu.roll(wide, 640 - 7 * 2**bit, 1), wide)
+    pick = one_hot(iota((256, 256), 0) == parameter_of(0))
+    return jnp.dot(wide[:, :256].astype(bf16), pick, preferred_element_type=f32)
+
+
+def last_table(flat):
+    lane = iota((256, 1), 0)
+    rest = lane % 80
+    row = rest % 8 * 27 + lane // 80 * 9 + rest // 8
+    valid = (lane < KROWS) & (rest < 72) & (rest % 8 < F)
+    source = jnp.where(valid, 67 + (row + 1) // 2, -1)
+    pick = one_hot(iota((256, 135), 1) == source)
+    both = jnp.dot(pick, flat.astype(bf16), preferred_element_type=f32)
+    mine = jnp.where((row + 1) % 2 == 1, both[:, CH:], both[:, :CH]).astype(bf16)
+    eye = one_hot(iota((CH, CH), 0) == iota((CH, CH), 1))
+    return lax.dot_general(eye, mine, NT, preferred_element_type=f32)
+
+
+def share_of(first, last, me):
+    of_first = me < CH
+    table = jnp.where(of_first, first, last)
+    place = iota((135, 1), 0)
+    flat = (me - CH) * 135 + place
+    row = flat // CH
+    lane = jnp.where(of_first, lane_of(place // F, place % F), lane_of(row % 27, row // 27))
+    pick = one_hot(iota((135, 256), 1) == lane)
+    values = sum(lax.dot_general(term, pick, NT, preferred_element_type=f32) for term in three_terms(table))
+    along = iota((CH, 135), 1)
+    unit = jnp.where(of_first, me, ((me - CH) * 135 + along) % CH)
+    return jnp.sum(jnp.where(iota((CH, 135), 0) == unit, values, 0.0), axis=0, keepdims=True)
 
 
 def device(group, column):
@@ -322,65 +375,104 @@
 
 
 def step_kernel(
-    block_ref, trainer_ref, out_ref, closure_in, closure_bias, trainer_row, first_in, last_in, brick,
-    new_fields, first_out, last_out,
-    wide_ref, padded, fresh, y_low, y_high, y_send, payload, window, north_rows, south_rows,
+    block_in, trainer_in, out_in, closure_in_, closure_bias_, trainer_row_, flat_in_, brick,
+    new_fields, share,
+    block_ref, trainer_ref, out_ref, closure_in, closure_bias, trainer_row, flat_in,
+    wide_ref, padded, y_low, y_high, y_send, payload, window, north_rows, south_rows, eddies, x_near_send, y_near_send, y_near,
     stack, hiddens, slopes, errors, pres, now_first, now_last, now_out,
     start, weights, grad, gathered, answer, running, delta,
-    load_sem, halo_send, halo_recv, store_sems, up_send, up_recv, down_send, down_recv, last_send, last_recv,
+    small_sems, load_sem, near_send, near_recv, halo_send, halo_recv,
+    up_send, up_recv, down_send, down_recv, last_send, last_recv,
 ):
     group = lax.axis_index("grp")
     column = lax.axis_index("gx") * lax.axis_size("gy") + lax.axis_index("gy")
     me = group * TRAINERS + column
     last_group = lax.axis_size("grp") - 1
+    sources = (block_in, trainer_in, out_in, closure_in_, closure_bias_, trainer_row_, flat_in_)
+    places_in = (block_ref, trainer_ref, out_ref, closure_in, closure_bias, trainer_row, flat_in)
+    small = [
+        pltpu.make_async_copy(source, to, small_sems.at[i]) for i, (source, to) in enumerate(zip(sources, places_in))
+    ]
+    for copy in small:
+        copy.start()
 
     def start_tables():
-        table = jnp.dot(first_in[...].astype(bf16), places(0), preferred_element_type=f32)
-        set_table(start, 0, table)
-        table = lax.dot_general(
-            last_in[...].astype(bf16), places(1), (((0,), (0,)), ((), ())), preferred_element_type=f32
-        )
-        set_table(start, 1, table)
+        flat = flat_in[...]
+        set_table(start, 0, first_table(flat))
+        set_table(start, 1, last_table(flat))
 
     @pl.when(group < last_group)
     def _():
         load = pltpu.make_async_copy(brick, padded.at[:, pl.ds(1, CX)], load_sem)
         load.start()
+        for copy in small:
+            copy.wait()
         gx, gy = lax.axis_index("gx"), lax.axis_index("gy")
         gx_size, gy_size = lax.axis_size("gx"), lax.axis_size("gy")
         x_next, x_last = lax.rem(gx + 1, gx_size), lax.rem(gx + gx_size - 1, gx_size)
         y_next, y_last = lax.rem(gy + 1, gy_size), lax.rem(gy + gy_size - 1, gy_size)
-        to_next_x = pltpu.make_async_remote_copy(
-            brick.at[:, CX - 1], padded.at[:, 0], halo_send.at[0], halo_recv.at[0], device_id={"gx": x_next}
-        )
-        to_last_x = pltpu.make_async_remote_copy(
-            brick.at[:, 0], padded.at[:, CX + 1], halo_send.at[1], halo_recv.at[1], device_id={"gx": x_last}
-        )
-        to_next_x.start()
-        to_last_x.start()
+        first_owner = group * TRAINERS
         load.wait()
-        for f in range(F):
-            y_send[0, f] = padded[f, 1 : CX + 1, CY - 1, :]
-            y_send[1, f] = padded[f, 1 : CX + 1, 0, :]
-        to_next_y = pltpu.make_async_remote_copy(
-            y_send.at[0], y_low, halo_send.at[2], halo_recv.at[2], device_id={"gy": y_next}
-        )
-        to_last_y = pltpu.make_async_remote_copy(
-            y_send.at[1], y_high, halo_send.at[3], halo_recv.at[3], device_id={"gy": y_last}
-        )
-        to_next_y.start()
-        to_last_y.start()
+        near = []
+        for side, to in enumerate((x_next, x_last)):
+            block = block_ref[first_owner + to * gy_size + gy]
+            plane = CX if side == 0 else 1
+            for f in range(F):
+                rows = jnp.where(block // 24 == 1, padded[f, plane, 16:, :], padded[f, plane, :16, :])
+                x_near_send[side, f] = cut(rows, block % 24)
+            copy = pltpu.make_async_remote_copy(
+                x_near_send.at[side],
+                window.at[:, 0 if side == 0 else CX + 1],
+                near_send.at[side],
+                near_recv.at[side],
+                device_id={"gx": to},
+            )
+            copy.start()
+            near.append(copy)
+        for side, to in enumerate((y_next, y_last)):
+            block = block_ref[first_owner + gx * gy_size + to]
+            line = CY - 1 if side == 0 else 0
+            for f in range(F):
+                rows = padded[f, 1 : CX + 1, line, :]
+                y_send[side, f] = rows
+                y_near_send[side, f] = cut(rows, block % 24)
+            copy = pltpu.make_async_remote_copy(
+                y_near_send.at[side],
+                y_near.at[side],
+                near_send.at[2 + side],
+                near_recv.at[2 + side],
+                device_id={"gy": to},
+            )
+            copy.start()
+            near.append(copy)
         spread_closure(closure_in, closure_bias, wide_ref)
+        own_block = block_ref[me]
+        own_windows(own_block, out_ref, padded, wide_ref, window, north_rows, south_rows, eddies)
         start_tables()
         same = (trainer_row[...] == trainer_ref[me]).astype(f32)
         count = jnp.sum(same, axis=1, keepdims=True)
         scale = 2.0 * (1.0 / (count * CELLS))
-        for copy in (to_next_x, to_last_x, to_next_y, to_last_y):
+        for copy in near:
             copy.wait()
-        cut_cube(block_ref[me], out_ref, padded, y_low, y_high, payload, wide_ref, window, north_rows, south_rows)
+        halos = [
+            pltpu.make_async_remote_copy(
+                brick.at[:, CX - 1], padded.at[:, 0], halo_send.at[0], halo_recv.at[0], device_id={"gx": x_next}
+            ),
+            pltpu.make_async_remote_copy(
+                brick.at[:, 0], padded.at[:, CX + 1], halo_send.at[1], halo_recv.at[1], device_id={"gx": x_last}
+            ),
+            pltpu.make_async_remote_copy(
+                y_send.at[0], y_low, halo_send.at[2], halo_recv.at[2], device_id={"gy": y_next}
+            ),
+            pltpu.make_async_remote_copy(
+                y_send.at[1], y_high, halo_send.at[3], halo_recv.at[3], device_id={"gy": y_last}
+            ),
+        ]
+        for copy in halos:
+            copy.start()
+        cut_cube(own_block, y_near, payload, window, north_rows, south_rows, eddies)
         build_stack(payload, stack, hiddens, errors)
         bounds = (0, 5, 10, CX)
-        stores = []
         for k in range(INNER):
             gradient(
                 scale, weights if k else start, payload, stack, hiddens, slopes, errors, pres,
@@ -399,23 +491,21 @@
                 return carry
 
             lax.fori_loop(0, TILES, send, 0, unroll=4)
-            stores.append(
-                evolve(
-                    bounds[k], bounds[k + 1], out_ref, padded, y_low, y_high, new_fields, wide_ref, fresh,
-                    store_sems.at[k],
-                )
-            )
+            if k == 0:
+                for copy in halos:
+                    copy.wait()
+            evolve(bounds[k], bounds[k + 1], out_ref, padded, y_low, y_high, new_fields, wide_ref)
             whole(grad, up_send).wait()
             if k < INNER - 1:
                 whole(weights, down_recv).wait()
-        for store in stores:
-            store.wait()
         whole(delta, last_recv).wait()
 
     @pl.when(group == last_group)
     def _():
         keep = pltpu.make_async_copy(brick, new_fields, load_sem)
         keep.start()
+        for copy in small:
+            copy.wait()
         start_tables()
         own_start = start[pl.ds(pl.multiple_of(column * 8, 8), 8), :]
         square = (OWNERS, OWNERS)
@@ -476,34 +566,30 @@
 
     values = delta[...]
     inverse = lax.rsqrt(jnp.sum(values * values) / NPARAM + norm_epsilon)
-    first_out[...] = sum(
-        lax.dot_general(term, places(0), NT, preferred_element_type=f32)
-        for term in three_terms(table_of(delta, 0) * inverse)
+    share[...] = inverse * share_of(table_of(delta, 0), table_of(delta, 1), me)
+
+
+def step_call(sample_block, sample_trainer, closure_out, closure_in, closure_bias, master, brick):
+    vmem = pl.BlockSpec(memory_space=pltpu.VMEM)
+    hbm = pl.BlockSpec(memory_space=pltpu.HBM)
+    dma = pltpu.SemaphoreType.DMA
+    operands = (
+        sample_block, sample_trainer, closure_out, closure_in.T, closure_bias.reshape(1, CH),
+        sample_trainer.reshape(1, OWNERS), master.reshape(135, 128), brick,
     )
-    last_out[...] = sum(
-        lax.dot_general(places(1), term, NT, preferred_element_type=f32)
-        for term in three_terms(table_of(delta, 1) * inverse)
-    )
-
-
-def step_call(sample_block, sample_trainer, closure_out, closure_in, closure_bias, first_in, last_in, brick):
-    smem = pl.BlockSpec(memory_space=pltpu.SMEM)
-    vmem = pl.BlockSpec(memory_space=pltpu.VMEM)
-    anywhere = pl.BlockSpec(memory_space=pl.ANY)
-    dma = pltpu.SemaphoreType.DMA
+    spaces = [pltpu.SMEM] * 3 + [pltpu.VMEM] * 4
     return pl.pallas_call(
         step_kernel,
         out_shape=(
             jax.ShapeDtypeStruct((F, CX, CY, CZ), f32),
-            jax.ShapeDtypeStruct((CH, 135), f32),
-            jax.ShapeDtypeStruct((135, CH), f32),
+            jax.ShapeDtypeStruct((1, 135), f32),
         ),
-        in_specs=[smem, smem, smem, vmem, vmem, vmem, vmem, vmem, anywhere],
-        out_specs=(anywhere, vmem, vmem),
-        scratch_shapes=[
+        in_specs=[hbm] * 8,
+        out_specs=(vmem, vmem),
+        scratch_shapes=[space(x.shape, x.dtype) for space, x in zip(spaces, operands)]
+        + [
             pltpu.VMEM((1024, 256), bf16),
             pltpu.VMEM((F, CX + 2, CY, CZ), f32),
-            pltpu.VMEM((F, CX, CY, CZ), f32),
             pltpu.VMEM((F, CX, CZ), f32),
             pltpu.VMEM((F, CX, CZ), f32),
             pltpu.VMEM((2, F, CX, CZ), f32),
@@ -511,6 +597,10 @@
             pltpu.VMEM((F, 18, 16, 128), f32),
             pltpu.VMEM((F, 16, 128), f32),
             pltpu.VMEM((F, 16, 128), f32),
+            pltpu.VMEM((4, 16, 512), f32),
+            pltpu.VMEM((2, F, 16, 128), f32),
+            pltpu.VMEM((2, F, 16, 128), f32),
+            pltpu.VMEM((2, F, 16, 128), f32),
             pltpu.VMEM((KROWS, WIDE), bf16),
             pltpu.VMEM((3 * CH, WIDE), bf16),
             pltpu.VMEM((CH, CELLS), f32),
@@ -526,10 +616,12 @@
             pltpu.VMEM((OWNERS * 8, 128), f32),
             pltpu.VMEM((8, OWNERS, 128), f32),
             pltpu.VMEM((TILES * 8, 128), f32),
+            dma((7,)),
             dma,
             dma((4,)),
             dma((4,)),
-            dma((INNER,)),
+            dma((4,)),
+            dma((4,)),
             dma,
             dma,
             dma,
@@ -537,34 +629,61 @@
             dma,
             dma,
         ],
-        compiler_params=pltpu.CompilerParams(vmem_limit_bytes=48 * 2**20, has_side_effects=True),
-    )(
-        sample_block, sample_trainer, closure_out, closure_in, closure_bias.reshape(1, CH),
-        sample_trainer.reshape(1, OWNERS), first_in, last_in, brick,
-    )
+        compiler_params=pltpu.CompilerParams(vmem_limit_bytes=60 * 2**20, has_side_effects=True),
+    )(*operands)
+
+
+def finish_kernel(made, share, momentum, master, new_fields, new_master, new_momentum, held, in_sems, out_sems):
+    into = [pltpu.make_async_copy(made.at[f], held.at[f], in_sems.at[f]) for f in range(F)]
+    out = [pltpu.make_async_copy(held.at[f], new_fields.at[f], out_sems.at[f]) for f in range(F)]
+    for copy in into:
+        copy.start()
+    columns = lax.axis_size("gy")
+    me = lax.axis_index("grp") * TRAINERS + lax.axis_index("gx") * columns + lax.axis_index("gy")
+    begin = me * 135
+    row = begin // 128
+
+    def mine(flat):
+        rows = [flat[pl.ds(jnp.minimum(row + i, 134), 1), :] for i in range(3)]
+        wide = jnp.broadcast_to(jnp.concatenate(rows, axis=1), (8, 384))
+        return pltpu.roll(wide, lax.rem(384 - begin % 128, 384), 1)[:1, :135]
+
+    momentum_share = momentum_decay * mine(momentum) + share[...]
+    new_momentum[...] = momentum_share
+    new_master[...] = mine(master) - outer_rate * momentum_share
+    for f in range(F):
+        into[f].wait()
+        out[f].start()
+    for f in range(F):
+        out[f].wait()
+
+
+def finish_call(made, share, momentum, master):
+    vmem = pl.BlockSpec(memory_space=pltpu.VMEM)
+    hbm = pl.BlockSpec(memory_space=pltpu.HBM)
+    part = jax.ShapeDtypeStruct((1, 135), f32)
+    return pl.pallas_call(
+        finish_kernel,
+        out_shape=(jax.ShapeDtypeStruct(made.shape, made.dtype), part, part),
+        in_specs=[hbm, vmem, vmem, vmem],
+        out_specs=(hbm, vmem, vmem),
+        scratch_shapes=[
+            pltpu.VMEM(made.shape, f32),
+            pltpu.SemaphoreType.DMA((F,)),
+            pltpu.SemaphoreType.DMA((F,)),
+        ],
+        compiler_params=pltpu.CompilerParams(vmem_limit_bytes=60 * 2**20),
+    )(made, share, momentum.reshape(135, 128), master.reshape(135, 128))
 
 
 def on_device(
     fields, closure_in, closure_bias, closure_out, master, momentum, sample_block, sample_trainer
 ):
-    column = lax.axis_index("gx") * lax.axis_size("gy") + lax.axis_index("gy")
-    me = lax.axis_index("grp") * TRAINERS + column
-    new_fields, first, last = step_call(
-        sample_block,
-        sample_trainer,
-        closure_out,
-        closure_in,
-        closure_bias,
-        master[:FIRST].reshape(CH, 135),
-        master[FIRST:].reshape(135, CH),
-        fields[0],
+    made, share = step_call(
+        sample_block, sample_trainer, closure_out, closure_in, closure_bias, master, fields[0]
     )
-    scaled = jnp.concatenate([first.reshape(FIRST), last.reshape(FIRST)])
-    size = NPARAM // (OWNERS + TRAINERS)
-    share = [lax.dynamic_slice_in_dim(whole_array, me * size, size) for whole_array in (momentum, master, scaled)]
-    new_momentum = momentum_decay * share[0] + share[2]
-    new_master = share[1] - outer_rate * new_momentum
-    return (new_fields[None], new_master, new_momentum)
+    new_fields, new_master, new_momentum = finish_call(made, share, momentum, master)
+    return (new_fields[None], new_master.reshape(135), new_momentum.reshape(135))
 
 
 def solution(mesh):

time: 95.6 us -> 82.7 us (0.87)
  local copies, waits for them, and re-layouts: 11.2 us -> 0 us
  other arithmetic: 1.38 us -> 0 us
    unnamed x12 -> x0, local copies, waits for them, and re-layouts: 9.74 us -> none
    pallas_call x1, Pallas kernels: 81.9 us -> 77.2 us  [step_call(): pl.pallas_call(step_kernel, out_shape=(jax.ShapeDtypeStruct((F, CX, CY, C...]
    pallas_call x0 -> x1, Pallas kernels: none -> 4.63 us  [finish_call(): pl.pallas_call(finish_kernel, out_shape=(jax.ShapeDtypeStruct(made.shape,...]
    sub x1 -> x0, other arithmetic: 1.38 us -> none  [on_device(): new_master = share[1] - outer_rate * new_momentum]
    slice x2 -> x0, local copies, waits for them, and re-layouts: 1.12 us -> none  [the longest x1 0.92 us: on_device(): master[FIRST:].reshape(135, CH)]
where the time goes in v3:
time: 82.7 us; the launch traced here: 82.5 us
  Pallas kernels  81.8 us (99%)
    pallas_call x1, Pallas kernels, step_call(): pl.pallas_call(step_kernel, out_shape=(jax.ShapeDtypeStruct((F, CX, CY, C...  77.2 us
    pallas_call x1, Pallas kernels, finish_call(): pl.pallas_call(finish_kernel, out_shape=(jax.ShapeDtypeStruct(made.shape,...  4.63 us

profile of v3, /device:TPU:1, one launch (start us, length us, event | category | flops | bytes accessed | tf_op | source)
XLA Modules:
  0.0 82.5 jit_solution(8776145642512961490)
XLA Ops:
  0.6 77.2 %shard_map.103 = (f32[5,16,32,384]{3,2,1,0:T(8,128)}, f32[1,135]{1,0:T(1,128)}) custom-call(s32[96]{0:T(128)} %block_in.1, s32[96]{0:T(128)} %trainer_in.1, f32[64]{0:T(128)} %out_in.1, f32[5,64]{1,0:T(8,128)} %bitcast.13, f32[1,64]{1,0:T(1,128)} %bitcast.15, s32[1,96]{1,0:T(1,128)} %bitcast.14, f32[135,128]{1,0:T(8,128)} %bitcast.10, f32[5,16,32,384]{3,2,1,0:T(8,128)} %bitcast.9), custom_call_target="tpu_custom_call" | custom-call | tf_op jit(solution)/shard_map/pallas_call | solution.py:581
  77.8 4.6 %shard_map.104 = (f32[5,16,32,384]{3,2,1,0:T(8,128)}, f32[1,135]{1,0:T(1,128)}, f32[1,135]{1,0:T(1,128)}) custom-call(f32[5,16,32,384]{3,2,1,0:T(8,128)} %get-tuple-element.8.made, f32[1,135]{1,0:T(1,128)} %get-tuple-element.9.share, f32[135,128]{1,0:T(8,128)} %bitcast.12, f32[135,128]{1,0:T(8,128)} %bitcast.11), custom_call_target="tpu_custom_call" | custom-call | tf_op jit(solution)/shard_map/pallas_call | solution.py:665

commit v4 on v3

--- a/solution.py
+++ b/solution.py
@@ -32,6 +32,7 @@
 momentum_decay = 0.9
 norm_epsilon = 1e-06
 f32 = jnp.float32
+MESH = pl.DeviceIdType.MESH
 bf16 = jnp.bfloat16
 NT = (((1,), (1,)), ((), ()))
 
@@ -370,6 +371,17 @@
     return {"grp": group, "gx": column // columns, "gy": lax.rem(column, columns)}
 
 
+def far_first(column, j):
+    def offset(t):
+        return (2 + 3 * t + 3 * (t // 2) + 2 * (t // 3)) % 4
+
+    gx, gy = column // 4, lax.rem(column, 4)
+    z = lax.rem(gx // 2 + offset(j // 8), 4)
+    y = lax.rem(gx + 1 - lax.rem(j, 2), 2)
+    x = lax.rem(gy + offset(lax.rem(j // 2, 4)), 4)
+    return (z * 2 + y) * 4 + x
+
+
 def whole(ref, sem):
     return pltpu.make_async_copy(ref, ref, sem)
 
@@ -382,12 +394,13 @@
     stack, hiddens, slopes, errors, pres, now_first, now_last, now_out,
     start, weights, grad, gathered, answer, running, delta,
     small_sems, load_sem, near_send, near_recv, halo_send, halo_recv,
-    up_send, up_recv, down_send, down_recv, last_send, last_recv,
+    up_send, up_recv, down_send, down_recv, last_send, last_recv, hand_send,
 ):
     group = lax.axis_index("grp")
     column = lax.axis_index("gx") * lax.axis_size("gy") + lax.axis_index("gy")
     me = group * TRAINERS + column
     last_group = lax.axis_size("grp") - 1
+    barrier = pltpu.get_barrier_semaphore()
     sources = (block_in, trainer_in, out_in, closure_in_, closure_bias_, trainer_row_, flat_in_)
     places_in = (block_ref, trainer_ref, out_ref, closure_in, closure_bias, trainer_row, flat_in)
     small = [
@@ -405,12 +418,27 @@
     def _():
         load = pltpu.make_async_copy(brick, padded.at[:, pl.ds(1, CX)], load_sem)
         load.start()
-        for copy in small:
-            copy.wait()
         gx, gy = lax.axis_index("gx"), lax.axis_index("gy")
         gx_size, gy_size = lax.axis_size("gx"), lax.axis_size("gy")
         x_next, x_last = lax.rem(gx + 1, gx_size), lax.rem(gx + gx_size - 1, gx_size)
         y_next, y_last = lax.rem(gy + 1, gy_size), lax.rem(gy + gy_size - 1, gy_size)
+
+        def greet(j, carry):
+            pl.semaphore_signal(barrier, 1, device_id=device(last_group, far_first(column, j)), device_id_type=MESH)
+            return carry
+
+        lax.fori_loop(0, TRAINERS, greet, 0)
+        for to in (x_next, x_last):
+            pl.semaphore_signal(barrier, 1, device_id={"gx": to}, device_id_type=MESH)
+        for to in (y_next, y_last):
+            pl.semaphore_signal(barrier, 1, device_id={"gy": to}, device_id_type=MESH)
+
+        before = lax.rem(group + last_group - 1, last_group)
+        pl.semaphore_signal(barrier, 1, device_id={"grp": before}, device_id_type=MESH)
+
+        for copy in small:
+            copy.wait()
+        spread_closure(closure_in, closure_bias, wide_ref)
         first_owner = group * TRAINERS
         load.wait()
         near = []
@@ -420,15 +448,15 @@
             for f in range(F):
                 rows = jnp.where(block // 24 == 1, padded[f, plane, 16:, :], padded[f, plane, :16, :])
                 x_near_send[side, f] = cut(rows, block % 24)
-            copy = pltpu.make_async_remote_copy(
-                x_near_send.at[side],
-                window.at[:, 0 if side == 0 else CX + 1],
-                near_send.at[side],
-                near_recv.at[side],
-                device_id={"gx": to},
+            near.append(
+                pltpu.make_async_remote_copy(
+                    x_near_send.at[side],
+                    window.at[:, 0 if side == 0 else CX + 1],
+                    near_send.at[side],
+                    near_recv.at[side],
+                    device_id={"gx": to},
+                )
             )
-            copy.start()
-            near.append(copy)
         for side, to in enumerate((y_next, y_last)):
             block = block_ref[first_owner + gx * gy_size + to]
             line = CY - 1 if side == 0 else 0
@@ -436,24 +464,18 @@
                 rows = padded[f, 1 : CX + 1, line, :]
                 y_send[side, f] = rows
                 y_near_send[side, f] = cut(rows, block % 24)
-            copy = pltpu.make_async_remote_copy(
-                y_near_send.at[side],
-                y_near.at[side],
-                near_send.at[2 + side],
-                near_recv.at[2 + side],
-                device_id={"gy": to},
+            near.append(
+                pltpu.make_async_remote_copy(
+                    y_near_send.at[side],
+                    y_near.at[side],
+                    near_send.at[2 + side],
+                    near_recv.at[2 + side],
+                    device_id={"gy": to},
+                )
             )
-            copy.start()
-            near.append(copy)
-        spread_closure(closure_in, closure_bias, wide_ref)
         own_block = block_ref[me]
         own_windows(own_block, out_ref, padded, wide_ref, window, north_rows, south_rows, eddies)
-        start_tables()
-        same = (trainer_row[...] == trainer_ref[me]).astype(f32)
-        count = jnp.sum(same, axis=1, keepdims=True)
-        scale = 2.0 * (1.0 / (count * CELLS))
-        for copy in near:
-            copy.wait()
+        pl.semaphore_wait(barrier, TRAINERS + 5)
         halos = [
             pltpu.make_async_remote_copy(
                 brick.at[:, CX - 1], padded.at[:, 0], halo_send.at[0], halo_recv.at[0], device_id={"gx": x_next}
@@ -468,8 +490,14 @@
                 y_send.at[1], y_high, halo_send.at[3], halo_recv.at[3], device_id={"gy": y_last}
             ),
         ]
-        for copy in halos:
+        for copy in near + halos:
             copy.start()
+        start_tables()
+        same = (trainer_row[...] == trainer_ref[me]).astype(f32)
+        count = jnp.sum(same, axis=1, keepdims=True)
+        scale = 2.0 * (1.0 / (count * CELLS))
+        for copy in near:
+            copy.wait()
         cut_cube(own_block, y_near, payload, window, north_rows, south_rows, eddies)
         build_stack(payload, stack, hiddens, errors)
         bounds = (0, 5, 10, CX)
@@ -480,7 +508,7 @@
             )
 
             def send(j, carry):
-                to = lax.rem(column + j, TILES)
+                to = far_first(column, j)
                 pltpu.make_async_remote_copy(
                     grad.at[pl.ds(pl.multiple_of(to * 8, 8), 8)],
                     gathered.at[pl.ds(pl.multiple_of(me * 8, 8), 8)],
@@ -500,10 +528,28 @@
                 whole(weights, down_recv).wait()
         whole(delta, last_recv).wait()
 
+        @pl.when(group == 0)
+        def _():
+            hand = pltpu.make_async_remote_copy(delta, delta, hand_send, last_recv, device_id={"grp": 1})
+            hand.start()
+            hand.wait_send()
+
     @pl.when(group == last_group)
     def _():
         keep = pltpu.make_async_copy(brick, new_fields, load_sem)
         keep.start()
+
+        def greet_owners(j, carry):
+            for g in range(OWNERS // TRAINERS):
+                pl.semaphore_signal(barrier, 1, device_id=device(g, far_first(column, j)), device_id_type=MESH)
+            return carry
+
+        def greet(j, carry):
+            pl.semaphore_signal(barrier, 1, device_id=device(last_group, far_first(column, j)), device_id_type=MESH)
+            return carry
+
+        lax.fori_loop(0, TRAINERS, greet_owners, 0)
+        lax.fori_loop(0, TRAINERS - 1, greet, 0)
         for copy in small:
             copy.wait()
         start_tables()
@@ -514,6 +560,7 @@
         down = jnp.sum(diagonal, axis=1, keepdims=True)
         same = (across == down).astype(f32).astype(bf16)
         running[...] = jnp.zeros_like(running)
+        pl.semaphore_wait(barrier, OWNERS + TRAINERS - 1)
         total = jnp.zeros((8, 128), f32)
         for k in range(INNER):
             whole(gathered, up_recv).wait()
@@ -533,7 +580,7 @@
                     answer[pl.ds(r, OWNERS, stride=8), :] = own_start[r : r + 1] - inner_rate * part
 
                 def send(j, carry):
-                    to = lax.rem(column + j, TRAINERS)
+                    to = far_first(column, j)
                     for g in range(OWNERS // TRAINERS):
                         pltpu.make_async_remote_copy(
                             answer.at[pl.ds(pl.multiple_of((g * TRAINERS + to) * 8, 8), 8)],
@@ -550,18 +597,20 @@
         own[...] = inner_rate * total
 
         def tell(j, carry):
-            to = lax.rem(me + j, OWNERS + TRAINERS)
-            pltpu.make_async_remote_copy(
-                own, own, last_send, last_recv, device_id=device(to // TRAINERS, lax.rem(to, TRAINERS))
-            ).start()
+            to = far_first(column, j)
+            for g in (0, last_group):
+                pltpu.make_async_remote_copy(own, own, last_send, last_recv, device_id=device(g, to)).start()
             return carry
 
-        lax.fori_loop(1, OWNERS + TRAINERS, tell, 0)
+        lax.fori_loop(0, TRAINERS - 1, tell, 0)
+        pltpu.make_async_remote_copy(own, own, last_send, last_recv, device_id=device(0, column)).start()
         others = delta.at[pl.ds(0, (TILES - 1) * 8)]
         whole(others, last_recv).wait()
-        for part in range(3):
-            whole(delta, last_send).wait()
+        hand = pltpu.make_async_remote_copy(delta, delta, hand_send, last_recv, device_id={"grp": 2})
+        hand.start()
+        whole(delta, last_send).wait()
         whole(others, last_send).wait()
+        hand.wait_send()
         keep.wait()
 
     values = delta[...]
@@ -628,8 +677,9 @@
             dma,
             dma,
             dma,
+            dma,
         ],
-        compiler_params=pltpu.CompilerParams(vmem_limit_bytes=60 * 2**20, has_side_effects=True),
+        compiler_params=pltpu.CompilerParams(vmem_limit_bytes=60 * 2**20, has_side_effects=True, collective_id=0),
     )(*operands)
 
 

time: 82.7 us -> 75.7 us (0.915)
  Pallas kernels: 81.8 us -> 74.9 us
    pallas_call x1, Pallas kernels: 77.2 us -> 70.2 us  [step_call(): pl.pallas_call(step_kernel, out_shape=(jax.ShapeDtypeStruct((F, CX, CY, C...]
where the time goes in v4:
time: 75.7 us; the launch traced here: 75.5 us
  Pallas kernels  74.9 us (99%)
    pallas_call x1, Pallas kernels, step_call(): pl.pallas_call(step_kernel, out_shape=(jax.ShapeDtypeStruct((F, CX, CY, C...  70.2 us
    pallas_call x1, Pallas kernels, finish_call(): pl.pallas_call(finish_kernel, out_shape=(jax.ShapeDtypeStruct(made.shape,...  4.63 us

profile of v4, /device:TPU:1, one launch (start us, length us, event | category | flops | bytes accessed | tf_op | source)
XLA Modules:
  0.0 75.5 jit_solution(3328520980581732111)
XLA Ops:
  0.6 70.2 %shard_map.103 = (f32[5,16,32,384]{3,2,1,0:T(8,128)}, f32[1,135]{1,0:T(1,128)}) custom-call(s32[96]{0:T(128)} %block_in.1, s32[96]{0:T(128)} %trainer_in.1, f32[64]{0:T(128)} %out_in.1, f32[5,64]{1,0:T(8,128)} %bitcast.13, f32[1,64]{1,0:T(1,128)} %bitcast.15, s32[1,96]{1,0:T(1,128)} %bitcast.14, f32[135,128]{1,0:T(8,128)} %bitcast.10, f32[5,16,32,384]{3,2,1,0:T(8,128)} %bitcast.9), custom_call_target="tpu_custom_call" | custom-call | tf_op jit(solution)/shard_map/pallas_call | solution.py:630
  70.9 4.6 %shard_map.104 = (f32[5,16,32,384]{3,2,1,0:T(8,128)}, f32[1,135]{1,0:T(1,128)}, f32[1,135]{1,0:T(1,128)}) custom-call(f32[5,16,32,384]{3,2,1,0:T(8,128)} %get-tuple-element.8.made, f32[1,135]{1,0:T(1,128)} %get-tuple-element.9.share, f32[135,128]{1,0:T(8,128)} %bitcast.12, f32[135,128]{1,0:T(8,128)} %bitcast.11), custom_call_target="tpu_custom_call" | custom-call | tf_op jit(solution)/shard_map/pallas_call | solution.py:715

commit v5 on v4

--- a/solution.py
+++ b/solution.py
@@ -136,7 +136,7 @@
     lax.fori_loop(0, 4, quarter, 0)
 
 
-def cut_cube(block, y_near, payload, window, north_rows, south_rows, eddies):
+def cut_cube(block, y_near, payload, window, north_rows, south_rows, eddies, cube_cells, cube_rows):
     upper_half = block // 24 == 1
     for f in range(F):
         south_rows[f] = jnp.where(upper_half, south_rows[f], y_near[0, f])
@@ -167,14 +167,14 @@
             tendency = advance(
                 center, east, west, north, south, upper, lower, eddy[:, j * 128 : (j + 1) * 128]
             )
-            both = jnp.concatenate(center + tendency, axis=0).astype(bf16)
-            flat = jnp.dot(both, unfold, preferred_element_type=f32)
-            flat = jnp.where(own_row, flat, 0.0).astype(bf16)
-            flat = jnp.dot(gather, flat, preferred_element_type=f32).astype(bf16)
-            payload[:, pl.ds(pl.multiple_of(x * 256, 256), 256)] = flat
+            cube_cells[x] = jnp.concatenate(center + tendency, axis=0).astype(bf16)
         return carry
 
     lax.fori_loop(0, 4, quarter, 0)
+    for x in range(CX):
+        flat = jnp.dot(cube_cells[x], unfold, preferred_element_type=f32)
+        cube_rows[:, x * 256 : (x + 1) * 256] = jnp.where(own_row, flat, 0.0).astype(bf16)
+    payload[...] = jnp.dot(gather, cube_rows[...], preferred_element_type=f32).astype(bf16)
 
 
 def evolve(begin, end, out_ref, padded, y_low, y_high, new_fields, wide_ref):
@@ -391,7 +391,7 @@
     new_fields, share,
     block_ref, trainer_ref, out_ref, closure_in, closure_bias, trainer_row, flat_in,
     wide_ref, padded, y_low, y_high, y_send, payload, window, north_rows, south_rows, eddies, x_near_send, y_near_send, y_near,
-    stack, hiddens, slopes, errors, pres, now_first, now_last, now_out,
+    cube_cells, cube_rows, stack, hiddens, slopes, errors, pres, now_first, now_last, now_out,
     start, weights, grad, gathered, answer, running, delta,
     small_sems, load_sem, near_send, near_recv, halo_send, halo_recv,
     up_send, up_recv, down_send, down_recv, last_send, last_recv, hand_send,
@@ -427,7 +427,7 @@
             pl.semaphore_signal(barrier, 1, device_id=device(last_group, far_first(column, j)), device_id_type=MESH)
             return carry
 
-        lax.fori_loop(0, TRAINERS, greet, 0)
+        lax.fori_loop(0, TRAINERS, greet, 0, unroll=True)
         for to in (x_next, x_last):
             pl.semaphore_signal(barrier, 1, device_id={"gx": to}, device_id_type=MESH)
         for to in (y_next, y_last):
@@ -498,7 +498,7 @@
         scale = 2.0 * (1.0 / (count * CELLS))
         for copy in near:
             copy.wait()
-        cut_cube(own_block, y_near, payload, window, north_rows, south_rows, eddies)
+        cut_cube(own_block, y_near, payload, window, north_rows, south_rows, eddies, cube_cells, cube_rows)
         build_stack(payload, stack, hiddens, errors)
         bounds = (0, 5, 10, CX)
         for k in range(INNER):
@@ -518,7 +518,7 @@
                 ).start()
                 return carry
 
-            lax.fori_loop(0, TILES, send, 0, unroll=4)
+            lax.fori_loop(0, TILES, send, 0, unroll=True)
             if k == 0:
                 for copy in halos:
                     copy.wait()
@@ -548,8 +548,8 @@
             pl.semaphore_signal(barrier, 1, device_id=device(last_group, far_first(column, j)), device_id_type=MESH)
             return carry
 
-        lax.fori_loop(0, TRAINERS, greet_owners, 0)
-        lax.fori_loop(0, TRAINERS - 1, greet, 0)
+        lax.fori_loop(0, TRAINERS, greet_owners, 0, unroll=True)
+        lax.fori_loop(0, TRAINERS - 1, greet, 0, unroll=True)
         for copy in small:
             copy.wait()
         start_tables()
@@ -591,7 +591,7 @@
                         ).start()
                     return carry
 
-                lax.fori_loop(0, TRAINERS, send, 0, unroll=2)
+                lax.fori_loop(0, TRAINERS, send, 0, unroll=True)
         whole(answer, down_send).wait()
         own = delta.at[pl.ds(pl.multiple_of(column * 8, 8), 8)]
         own[...] = inner_rate * total
@@ -602,7 +602,7 @@
                 pltpu.make_async_remote_copy(own, own, last_send, last_recv, device_id=device(g, to)).start()
             return carry
 
-        lax.fori_loop(0, TRAINERS - 1, tell, 0)
+        lax.fori_loop(0, TRAINERS - 1, tell, 0, unroll=True)
         pltpu.make_async_remote_copy(own, own, last_send, last_recv, device_id=device(0, column)).start()
         others = delta.at[pl.ds(0, (TILES - 1) * 8)]
         whole(others, last_recv).wait()
@@ -626,6 +626,7 @@
         sample_block, sample_trainer, closure_out, closure_in.T, closure_bias.reshape(1, CH),
         sample_trainer.reshape(1, OWNERS), master.reshape(135, 128), brick,
     )
+    operands = [pltpu.with_memory_space_constraint(x, pltpu.HBM) for x in operands]
     spaces = [pltpu.SMEM] * 3 + [pltpu.VMEM] * 4
     return pl.pallas_call(
         step_kernel,
@@ -650,6 +651,8 @@
             pltpu.VMEM((2, F, 16, 128), f32),
             pltpu.VMEM((2, F, 16, 128), f32),
             pltpu.VMEM((2, F, 16, 128), f32),
+            pltpu.VMEM((CX, 160, 128), bf16),
+            pltpu.VMEM((160, CELLS), bf16),
             pltpu.VMEM((KROWS, WIDE), bf16),
             pltpu.VMEM((3 * CH, WIDE), bf16),
             pltpu.VMEM((CH, CELLS), f32),
@@ -679,15 +682,12 @@
             dma,
             dma,
         ],
-        compiler_params=pltpu.CompilerParams(vmem_limit_bytes=60 * 2**20, has_side_effects=True, collective_id=0),
+        compiler_params=pltpu.CompilerParams(vmem_limit_bytes=50 * 2**20, has_side_effects=True, collective_id=0),
     )(*operands)
 
 
-def finish_kernel(made, share, momentum, master, new_fields, new_master, new_momentum, held, in_sems, out_sems):
-    into = [pltpu.make_async_copy(made.at[f], held.at[f], in_sems.at[f]) for f in range(F)]
-    out = [pltpu.make_async_copy(held.at[f], new_fields.at[f], out_sems.at[f]) for f in range(F)]
-    for copy in into:
-        copy.start()
+def finish_kernel(made, share, momentum, master, new_fields, new_master, new_momentum, in_sems, out_sems):
+    out = [pltpu.make_async_copy(made.at[f], new_fields.at[f], out_sems.at[f]) for f in range(F)]
     columns = lax.axis_size("gy")
     me = lax.axis_index("grp") * TRAINERS + lax.axis_index("gx") * columns + lax.axis_index("gy")
     begin = me * 135
@@ -702,7 +702,6 @@
     new_momentum[...] = momentum_share
     new_master[...] = mine(master) - outer_rate * momentum_share
     for f in range(F):
-        into[f].wait()
         out[f].start()
     for f in range(F):
         out[f].wait()
@@ -715,14 +714,13 @@
     return pl.pallas_call(
         finish_kernel,
         out_shape=(jax.ShapeDtypeStruct(made.shape, made.dtype), part, part),
-        in_specs=[hbm, vmem, vmem, vmem],
+        in_specs=[vmem, vmem, vmem, vmem],
         out_specs=(hbm, vmem, vmem),
         scratch_shapes=[
-            pltpu.VMEM(made.shape, f32),
             pltpu.SemaphoreType.DMA((F,)),
             pltpu.SemaphoreType.DMA((F,)),
         ],
-        compiler_params=pltpu.CompilerParams(vmem_limit_bytes=60 * 2**20),
+        compiler_params=pltpu.CompilerParams(vmem_limit_bytes=6 * 2**20),
     )(made, share, momentum.reshape(135, 128), master.reshape(135, 128))
 
 

time: 75.7 us -> 69.8 us (0.922)
  Pallas kernels: 74.9 us -> 68.8 us
    pallas_call x1, Pallas kernels: 70.2 us -> 66.2 us  [step_call(): pl.pallas_call(step_kernel, out_shape=(jax.ShapeDtypeStruct((F, CX, CY, C...]
    pallas_call x1, Pallas kernels: 4.63 us -> 2.59 us  [finish_call(): pl.pallas_call(finish_kernel, out_shape=(jax.ShapeDtypeStruct(made.shape,...]
where the time goes in v5:
time: 69.8 us; the launch traced here: 69.7 us
  Pallas kernels  68.8 us (99%)
  between operations  0.83 us (1%)
    pallas_call x1, Pallas kernels, step_call(): pl.pallas_call(step_kernel, out_shape=(jax.ShapeDtypeStruct((F, CX, CY, C...  66.2 us
    pallas_call x1, Pallas kernels, finish_call(): pl.pallas_call(finish_kernel, out_shape=(jax.ShapeDtypeStruct(made.shape,...  2.59 us

profile of v5, /device:TPU:1, one launch (start us, length us, event | category | flops | bytes accessed | tf_op | source)
XLA Modules:
  0.0 69.7 jit_solution(11968763544905190795)
XLA Ops:
  0.6 0.0 copy-start.1
  0.6 0.0 copy-start
  0.7 66.2 %shard_map.103 = (f32[5,16,32,384]{3,2,1,0:T(8,128)S(1)}, f32[1,135]{1,0:T(1,128)S(1)}) custom-call(s32[96]{0:T(128)} %block_in.1, s32[96]{0:T(128)} %trainer_in.1, f32[64]{0:T(128)} %out_in.1, f32[5,64]{1,0:T(8,128)} %bitcast.13, f32[1,64]{1,0:T(1,128)} %bitcast.15, s32[1,96]{1,0:T(1,128)} %bitcast.14, f32[135,128]{1,0:T(8,128)} %bitcast.9, ...), custom_call_target="tpu_custom_call" | custom-call | tf_op jit(solution)/shard_map/pallas_call | solution.py:631
  66.9 0.0 copy-done.1
  66.9 0.0 copy-done
  66.9 2.6 %shard_map.104 = (f32[5,16,32,384]{3,2,1,0:T(8,128)}, f32[1,135]{1,0:T(1,128)}, f32[1,135]{1,0:T(1,128)}) custom-call(f32[5,16,32,384]{3,2,1,0:T(8,128)S(1)} %get-tuple-element.8.made, f32[1,135]{1,0:T(1,128)S(1)} %get-tuple-element.9.share, f32[135,128]{1,0:T(8,128)S(1)} %bitcast.11, f32[135,128]{1,0:T(8,128)S(1)} %bitcast.10), custom_call_target="tpu_custom_call" | custom-call | tf_op jit(solution)/shard_map/pallas_call | solution.py:714
Async XLA Ops:
  0.6 66.3 %copy-start.1 = (f32[17280]{0:T(1024)S(1)}, f32[17280]{0:T(1024)}, u32[]{:S(2)}) copy-start(f32[17280]{0:T(1024)} %param.13) | copy-start | bytes 207364
  0.6 66.3 %copy-start = (f32[17280]{0:T(1024)S(1)}, f32[17280]{0:T(1024)}, u32[]{:S(2)}) copy-start(f32[17280]{0:T(1024)} %param.12) | copy-start | bytes 207364

commit v6 on v5

--- a/solution.py
+++ b/solution.py
@@ -259,7 +259,7 @@
     tiles[layer * 128 + 64 : layer * 128 + 128, :] = table[:, 128:]
 
 
-def gradient(scale, weights, payload, stack, hiddens, slopes, errors, pres, now_first, now_last, now_out, grad):
+def gradient(scale, weights, payload, stack, hiddens, slopes, errors, pres, now_first, now_last, now_out, grad, send):
     eye = (iota((KROWS, KROWS), 0) == iota((KROWS, KROWS), 1)).astype(f32).astype(bf16)
     now_first[...] = table_of(weights, 0)[:, :KROWS].astype(bf16)
     last = table_of(weights, 1)[:, :KROWS].astype(bf16)
@@ -295,16 +295,17 @@
         for x_step in STEPS:
             at = o + BASE * x_step
             errors[(x_step + 1) * 80 : (x_step + 2) * 80, at : at + CHUNK] = rows
+    cells = slice(BASE, BASE + CELLS)
+    spare = jnp.zeros((CH, 256 - KROWS), f32)
     for i in range(0, CELLS, CHUNK):
         o = BASE + i
         back = jnp.dot(now_last[...], errors[:, o : o + CHUNK], preferred_element_type=f32)
         pres[:, i : i + CHUNK] = (back * slopes[:, i : i + CHUNK]).astype(bf16)
-    cells = slice(BASE, BASE + CELLS)
-    spare = jnp.zeros((CH, 256 - KROWS), f32)
     first = lax.dot_general(pres[...], stack[:, cells], NT, preferred_element_type=f32)
     set_table(grad, 0, jnp.concatenate([first, spare], axis=1))
     last = lax.dot_general(hiddens[CH : 2 * CH, cells], errors[:, cells], NT, preferred_element_type=f32)
     set_table(grad, 1, jnp.concatenate([last, spare], axis=1))
+    send()
 
 
 def three_terms(values):
@@ -352,18 +353,20 @@
     return lax.dot_general(eye, mine, NT, preferred_element_type=f32)
 
 
-def share_of(first, last, me):
+def share_map(me, share_pick, share_unit):
     of_first = me < CH
-    table = jnp.where(of_first, first, last)
-    place = iota((135, 1), 0)
-    flat = (me - CH) * 135 + place
-    row = flat // CH
+    place = iota((144, 1), 0)
+    row = ((me - CH) * 135 + place) // CH
     lane = jnp.where(of_first, lane_of(place // F, place % F), lane_of(row % 27, row // 27))
-    pick = one_hot(iota((135, 256), 1) == lane)
-    values = sum(lax.dot_general(term, pick, NT, preferred_element_type=f32) for term in three_terms(table))
-    along = iota((CH, 135), 1)
+    share_pick[...] = one_hot((iota((144, 256), 1) == lane) & (place < 135))
+    along = iota((CH, 144), 1)
     unit = jnp.where(of_first, me, ((me - CH) * 135 + along) % CH)
-    return jnp.sum(jnp.where(iota((CH, 135), 0) == unit, values, 0.0), axis=0, keepdims=True)
+    share_unit[...] = (iota((CH, 144), 0) == unit).astype(f32)
+
+
+def share_of(table, share_pick, share_unit):
+    values = sum(lax.dot_general(term, share_pick[...], NT, preferred_element_type=f32) for term in three_terms(table))
+    return jnp.sum(values * share_unit[...], axis=0, keepdims=True)[:, :135]
 
 
 def device(group, column):
@@ -392,7 +395,7 @@
     block_ref, trainer_ref, out_ref, closure_in, closure_bias, trainer_row, flat_in,
     wide_ref, padded, y_low, y_high, y_send, payload, window, north_rows, south_rows, eddies, x_near_send, y_near_send, y_near,
     cube_cells, cube_rows, stack, hiddens, slopes, errors, pres, now_first, now_last, now_out,
-    start, weights, grad, gathered, answer, running, delta,
+    start, weights, grad, gathered, answer, running, delta, share_pick, share_unit,
     small_sems, load_sem, near_send, near_recv, halo_send, halo_recv,
     up_send, up_recv, down_send, down_recv, last_send, last_recv, hand_send,
 ):
@@ -413,6 +416,7 @@
         flat = flat_in[...]
         set_table(start, 0, first_table(flat))
         set_table(start, 1, last_table(flat))
+        share_map(me, share_pick, share_unit)
 
     @pl.when(group < last_group)
     def _():
@@ -490,7 +494,7 @@
                 y_send.at[1], y_high, halo_send.at[3], halo_recv.at[3], device_id={"gy": y_last}
             ),
         ]
-        for copy in near + halos:
+        for copy in near:
             copy.start()
         start_tables()
         same = (trainer_row[...] == trainer_ref[me]).astype(f32)
@@ -500,14 +504,10 @@
             copy.wait()
         cut_cube(own_block, y_near, payload, window, north_rows, south_rows, eddies, cube_cells, cube_rows)
         build_stack(payload, stack, hiddens, errors)
-        bounds = (0, 5, 10, CX)
-        for k in range(INNER):
-            gradient(
-                scale, weights if k else start, payload, stack, hiddens, slopes, errors, pres,
-                now_first, now_last, now_out, grad,
-            )
-
-            def send(j, carry):
+        bounds = (0, 0, 8, CX)
+
+        def send_layer():
+            for j in range(TILES):
                 to = far_first(column, j)
                 pltpu.make_async_remote_copy(
                     grad.at[pl.ds(pl.multiple_of(to * 8, 8), 8)],
@@ -516,13 +516,20 @@
                     up_recv,
                     device_id=device(last_group, to),
                 ).start()
-                return carry
-
-            lax.fori_loop(0, TILES, send, 0, unroll=True)
+
+        for k in range(INNER):
+            gradient(
+                scale, weights if k else start, payload, stack, hiddens, slopes, errors, pres,
+                now_first, now_last, now_out, grad, send_layer,
+            )
             if k == 0:
                 for copy in halos:
+                    copy.start()
+            if k == 1:
+                for copy in halos:
                     copy.wait()
-            evolve(bounds[k], bounds[k + 1], out_ref, padded, y_low, y_high, new_fields, wide_ref)
+            if k:
+                evolve(bounds[k], bounds[k + 1], out_ref, padded, y_low, y_high, new_fields, wide_ref)
             whole(grad, up_send).wait()
             if k < INNER - 1:
                 whole(weights, down_recv).wait()
@@ -558,26 +565,25 @@
         across = jnp.broadcast_to(trainer_row[...].astype(f32), square)
         diagonal = jnp.where(iota(square, 0) == iota(square, 1), across, 0.0)
         down = jnp.sum(diagonal, axis=1, keepdims=True)
-        same = (across == down).astype(f32).astype(bf16)
+        same = jnp.concatenate([(across == down).astype(f32), jnp.ones((8, OWNERS), f32)], axis=0).astype(bf16)
+        ones = jnp.ones((8, OWNERS), bf16)
         running[...] = jnp.zeros_like(running)
+
+        def summed(rows):
+            wide = jnp.concatenate([gathered[pl.ds(r, OWNERS, stride=8), :] for r in range(8)], axis=1)
+            return sum(jnp.dot(rows, term, preferred_element_type=f32) for term in three_terms(wide))
+
         pl.semaphore_wait(barrier, OWNERS + TRAINERS - 1)
-        total = jnp.zeros((8, 128), f32)
         for k in range(INNER):
             whole(gathered, up_recv).wait()
-
-            def add(o, total):
-                return total + gathered[pl.ds(pl.multiple_of(o * 8, 8), 8), :]
-
-            total = lax.fori_loop(0, OWNERS, add, total, unroll=8)
             if k < INNER - 1:
                 if k:
                     whole(answer, down_send).wait()
+                part = running[...] + summed(same)
+                running[...] = part
                 for r in range(8):
-                    terms = three_terms(gathered[pl.ds(r, OWNERS, stride=8), :])
-                    part = sum(jnp.dot(same, term, preferred_element_type=f32) for term in terms)
-                    part = running[r] + part
-                    running[r] = part
-                    answer[pl.ds(r, OWNERS, stride=8), :] = own_start[r : r + 1] - inner_rate * part
+                    lanes = slice(r * 128, (r + 1) * 128)
+                    answer[pl.ds(r, OWNERS, stride=8), :] = own_start[r : r + 1] - inner_rate * part[:OWNERS, lanes]
 
                 def send(j, carry):
                     to = far_first(column, j)
@@ -592,9 +598,9 @@
                     return carry
 
                 lax.fori_loop(0, TRAINERS, send, 0, unroll=True)
-        whole(answer, down_send).wait()
         own = delta.at[pl.ds(pl.multiple_of(column * 8, 8), 8)]
-        own[...] = inner_rate * total
+        part = running[OWNERS : OWNERS + 8] + summed(ones)
+        own[...] = inner_rate * jnp.concatenate([part[:1, r * 128 : (r + 1) * 128] for r in range(8)], axis=0)
 
         def tell(j, carry):
             to = far_first(column, j)
@@ -605,6 +611,7 @@
         lax.fori_loop(0, TRAINERS - 1, tell, 0, unroll=True)
         pltpu.make_async_remote_copy(own, own, last_send, last_recv, device_id=device(0, column)).start()
         others = delta.at[pl.ds(0, (TILES - 1) * 8)]
+        whole(answer, down_send).wait()
         whole(others, last_recv).wait()
         hand = pltpu.make_async_remote_copy(delta, delta, hand_send, last_recv, device_id={"grp": 2})
         hand.start()
@@ -615,7 +622,8 @@
 
     values = delta[...]
     inverse = lax.rsqrt(jnp.sum(values * values) / NPARAM + norm_epsilon)
-    share[...] = inverse * share_of(table_of(delta, 0), table_of(delta, 1), me)
+    table = jnp.where(me < CH, table_of(delta, 0), table_of(delta, 1))
+    share[...] = inverse * share_of(table, share_pick, share_unit)
 
 
 def step_call(sample_block, sample_trainer, closure_out, closure_in, closure_bias, master, brick):
@@ -666,8 +674,10 @@
             pltpu.VMEM((TILES * 8, 128), f32),
             pltpu.VMEM((OWNERS * 8, 128), f32),
             pltpu.VMEM((OWNERS * 8, 128), f32),
-            pltpu.VMEM((8, OWNERS, 128), f32),
+            pltpu.VMEM((OWNERS + 8, 1024), f32),
             pltpu.VMEM((TILES * 8, 128), f32),
+            pltpu.VMEM((144, 256), bf16),
+            pltpu.VMEM((CH, 144), f32),
             dma((7,)),
             dma,
             dma((4,)),

time: 69.8 us -> 67.1 us (0.961)
  Pallas kernels: 68.8 us -> 66.2 us
    pallas_call x1, Pallas kernels: 66.2 us -> 63.6 us  [step_call(): pl.pallas_call(step_kernel, out_shape=(jax.ShapeDtypeStruct((F, CX, CY, C...]
where the time goes in v6:
time: 67.1 us; the launch traced here: 67 us
  Pallas kernels  66.2 us (99%)
  between operations  0.83 us (1%)
    pallas_call x1, Pallas kernels, step_call(): pl.pallas_call(step_kernel, out_shape=(jax.ShapeDtypeStruct((F, CX, CY, C...  63.6 us
    pallas_call x1, Pallas kernels, finish_call(): pl.pallas_call(finish_kernel, out_shape=(jax.ShapeDtypeStruct(made.shape,...  2.59 us

profile of v6, /device:TPU:1, one launch (start us, length us, event | category | flops | bytes accessed | tf_op | source)
XLA Modules:
  0.0 67.0 jit_solution(8230604043170621325)
XLA Ops:
  0.6 0.0 copy-start.1
  0.6 0.0 copy-start
  0.7 63.6 %shard_map.103 = (f32[5,16,32,384]{3,2,1,0:T(8,128)S(1)}, f32[1,135]{1,0:T(1,128)S(1)}) custom-call(s32[96]{0:T(128)} %block_in.1, s32[96]{0:T(128)} %trainer_in.1, f32[64]{0:T(128)} %out_in.1, f32[5,64]{1,0:T(8,128)} %bitcast.13, f32[1,64]{1,0:T(1,128)} %bitcast.15, s32[1,96]{1,0:T(1,128)} %bitcast.14, f32[135,128]{1,0:T(8,128)} %bitcast.9, ...), custom_call_target="tpu_custom_call" | custom-call | tf_op jit(solution)/shard_map/pallas_call | solution.py:639
  64.2 0.0 copy-done.1
  64.3 0.0 copy-done
  64.3 2.6 %shard_map.104 = (f32[5,16,32,384]{3,2,1,0:T(8,128)}, f32[1,135]{1,0:T(1,128)}, f32[1,135]{1,0:T(1,128)}) custom-call(f32[5,16,32,384]{3,2,1,0:T(8,128)S(1)} %get-tuple-element.8.made, f32[1,135]{1,0:T(1,128)S(1)} %get-tuple-element.9.share, f32[135,128]{1,0:T(8,128)S(1)} %bitcast.11, f32[135,128]{1,0:T(8,128)S(1)} %bitcast.10), custom_call_target="tpu_custom_call" | custom-call | tf_op jit(solution)/shard_map/pallas_call | solution.py:724
Async XLA Ops:
  0.6 63.6 %copy-start.1 = (f32[17280]{0:T(1024)S(1)}, f32[17280]{0:T(1024)}, u32[]{:S(2)}) copy-start(f32[17280]{0:T(1024)} %param.13) | copy-start | bytes 207364
  0.6 63.6 %copy-start = (f32[17280]{0:T(1024)S(1)}, f32[17280]{0:T(1024)}, u32[]{:S(2)}) copy-start(f32[17280]{0:T(1024)} %param.12) | copy-start | bytes 207364
